TPU v7x, 512 devices: a whole 4x4x16 slice. The times are simulated.
512 devices in a mesh: lon: 32 (over z, y_lo), lat: 4 (over x), lev: 4 (over y_hi, core).
Axes of the slice: x: 4, y: 4 (y_hi: 2, y_lo: 2; y = y_hi * 2 + y_lo), z: 16, core: 2. Of those that a mesh axis runs over, the one named last changes fastest.
Arguments:
- adjoint_in: float32 [8, 16, 16, 8192], P(None, 'lev', 'lat', 'lon'), may hold values from -6 to 6
- courant_lon: float32 [16, 16, 8192], P('lev', 'lat', 'lon'), may hold values from 0.05 to 0.45
- courant_lat: float32 [16, 16, 8192], P('lev', 'lat', 'lon'), may hold values from 0.05 to 0.25
- horiz_diff: float32 [8], replicated, may hold values from 0.01 to 0.06
- vert_diff: float32 [16], replicated, may hold values from 0.01 to 0.1
- innovations: bfloat16 [8192, 8, 16, 128], P(('lon', 'lat'), None, 'lev'), may hold values from -6 to 6
- obs_operator: bfloat16 [8192, 128, 256], P(('lon', 'lat')), may hold values from -0.5 to 0.5
- owner_tile: int32 [8192, 1], P(('lon', 'lat')), may hold values from 0 to 31; in each aligned block of 64 rows (0 to 63, 64 to 127, ...) at most 4 rows name the same one
- block_row: int32 [8192], P(('lon', 'lat')), may hold values from 0 to 3
- obs_count: int32 [8192], P(('lon', 'lat')), may hold values from 1 to 128
Outputs:
- adjoint_out: float32 [8, 16, 16, 8192], P(None, 'lev', 'lat', 'lon')
Inputs may be any that keep to these rules, and one draw needn't show every extreme that they name: `owner_tile`: among the 64 blocks of one device at most 4 name the same longitude tile; in some device exactly 4 do.
All inputs are finite; a program needn't handle non-finite values.
Results may differ from a plain program's by a relative error of at most 0.002.
The roundings to bfloat16 on the way count: a program that leaves them out, or rounds other values in their place, can miss the bound.
Values may be sent and summed in bfloat16 or wider, within the bound.
A program may use at most 64 MiB of HBM per device.

v0:
```python
import jax
import jax.numpy as jnp
from jax import lax
from jax.sharding import PartitionSpec as P

STEPS = 3


def extended_2(block, sides, width, periodic):
    for axis, dim in sides:
        count = lax.axis_size(axis)
        forward = [(i, i + 1) for i in range(count - 1)]
        if periodic:
            forward.append((count - 1, 0))
        backward = [(target, source) for source, target in forward]
        low = lax.ppermute(
            lax.slice_in_dim(block, block.shape[dim] - width, None, axis=dim), axis, forward
        )
        high = lax.ppermute(lax.slice_in_dim(block, 0, width, axis=dim), axis, backward)
        block = jnp.concatenate([low, block, high], axis=dim)
    return block


def widen(field, rim_width):
    beside_all = extended_2(field, (("lon", 3),), rim_width, True)
    return extended_2(beside_all, (("lat", 2), ("lev", 1)), rim_width, False)


def sweep(
    extended,
    wind_pair,
    horiz_diff,
    vert_diff,
    rim_width,
    lev_first,
    lat_first,
    level_total,
    lat_total,
):
    out_rim = rim_width - 1
    lev_glob = lev_first - out_rim + jnp.arange(extended.shape[1] - 2, dtype=jnp.int32)
    lat_glob = lat_first - out_rim + jnp.arange(extended.shape[2] - 2, dtype=jnp.int32)
    level_ids = jnp.arange(level_total, dtype=jnp.int32)
    coef_up = jnp.sum(
        jnp.where(
            (lev_glob[:, None] == level_ids[None, :]) & (level_ids[None, :] < level_total - 1),
            vert_diff[None, :],
            0.0,
        ),
        axis=1,
    )
    coef_down = jnp.sum(
        jnp.where(lev_glob[:, None] - 1 == level_ids[None, :], vert_diff[None, :], 0.0), axis=1
    )
    inside = (
        ((lev_glob >= 0) & (lev_glob < level_total))[:, None]
        & ((lat_glob >= 0) & (lat_glob < lat_total))[None, :]
    ).astype(jnp.float32)
    east_flux = wind_pair[0][None] * extended
    north_flux = wind_pair[1][None] * extended
    centre = extended[:, 1:-1, 1:-1, 1:-1]
    result = centre - east_flux[:, 1:-1, 1:-1, 1:-1] - north_flux[:, 1:-1, 1:-1, 1:-1]
    result = result + east_flux[:, 1:-1, 1:-1, 2:] + north_flux[:, 1:-1, 2:, 1:-1]
    spread = (
        extended[:, 1:-1, 1:-1, 2:]
        + extended[:, 1:-1, 1:-1, :-2]
        + extended[:, 1:-1, 2:, 1:-1]
        + extended[:, 1:-1, :-2, 1:-1]
        - 4.0 * centre
    )
    result = result + horiz_diff[:, None, None, None] * spread
    result = result + coef_up[None, :, None, None] * (extended[:, 2:, 1:-1, 1:-1] - centre)
    result = result + coef_down[None, :, None, None] * (extended[:, :-2, 1:-1, 1:-1] - centre)
    return result * inside[None, :, :, None]


def on_device(
    adjoint_in,
    courant_lon,
    courant_lat,
    horiz_diff,
    vert_diff,
    innovations,
    obs_operator,
    owner_tile,
    block_row,
    obs_count,
):
    num_fields = adjoint_in.shape[0]
    lev_cells = adjoint_in.shape[1]
    lat_cells = adjoint_in.shape[2]
    lon_cells = adjoint_in.shape[3]
    num_blocks = innovations.shape[0]
    obs_rows = innovations.shape[3]
    level_total = lev_cells * lax.axis_size("lev")
    lat_total = lat_cells * lax.axis_size("lat")
    lev_first = lax.axis_index("lev") * lev_cells
    lat_first = lax.axis_index("lat") * lat_cells
    observed = jnp.arange(obs_rows, dtype=jnp.int32)[None, :] < obs_count[:, None]
    masked = jnp.where(observed[:, None, None, :], innovations, jnp.zeros((), jnp.bfloat16))
    masked = masked.reshape(num_blocks, num_fields * lev_cells, obs_rows)
    products = jnp.einsum(
        "bvo,boc->bvc", masked, obs_operator, preferred_element_type=jnp.float32
    ).astype(jnp.bfloat16)
    flattened = products.reshape(num_blocks, num_fields * lev_cells * lon_cells)
    dest_tile = owner_tile[:, 0]
    target = dest_tile * lat_cells + block_row
    picks = (
        jnp.arange(lax.axis_size("lon") * lat_cells, dtype=jnp.int32)[:, None] == target[None, :]
    ).astype(jnp.bfloat16)
    obs_sum = lax.psum_scatter(
        jnp.dot(picks, flattened, preferred_element_type=jnp.float32),
        "lon",
        scatter_dimension=0,
        tiled=True,
    )
    obs_gradient = obs_sum.reshape(lat_cells, num_fields, lev_cells, lon_cells).transpose(
        1, 2, 0, 3
    )
    wind_pair = jnp.stack([courant_lon, courant_lat])
    joined = jnp.concatenate([adjoint_in, wind_pair], axis=0)
    widened = widen(joined, 1)
    wind_wide = widened[num_fields:]
    adjoint = sweep(
        widened[:num_fields],
        wind_wide,
        horiz_diff,
        vert_diff,
        1,
        lev_first,
        lat_first,
        level_total,
        lat_total,
    )
    for sub_step in range(STEPS - 1):
        adjoint = sweep(
            widen(adjoint, 1),
            wind_wide,
            horiz_diff,
            vert_diff,
            1,
            lev_first,
            lat_first,
            level_total,
            lat_total,
        )
    return adjoint + obs_gradient


def solution(mesh):
    in_specs = (
        P(None, "lev", "lat", "lon"),
        P("lev", "lat", "lon"),
        P("lev", "lat", "lon"),
        P(),
        P(),
        P(("lon", "lat"), None, "lev", None),
        P(("lon", "lat"), None, None),
        P(("lon", "lat"), None),
        P(("lon", "lat")),
        P(("lon", "lat")),
    )
    out_specs = P(None, "lev", "lat", "lon")
    return jax.shard_map(
        on_device, mesh=mesh, in_specs=in_specs, out_specs=out_specs, check_vma=False
    )
```

profile of v0, /device:TPU:6, one launch (start us, length us, event | category | flops | bytes accessed | tf_op | source)
XLA Modules:
  0.0 317.4 jit_solution(7469303934517993894)
XLA Ops:
  7.3 1.3 broadcast_select_fusion
  8.6 2.9 convolution_convert_fusion
  12.2 2.7 fusion.52
  15.1 12.4 %collective-permute-start.1 = (f32[10,4,4,1]{3,2,1,0:T(4,128)S(1)}, f32[10,4,4,1]{3,2,1,0:T(4,128)S(1)}, u32[]{:S(2)}, u32[]{:S(2)}) collective-permute-start(f32[10,4,4,1]{3,2,1,0:T(4,128)S(1)} %get-tuple-element.28), channel_id=1, source_target_pairs={{16,0},{32,16},{48,32},{64,48},{80,64},{96,80},{112,96},{128,112},... | collective-permute-start | bytes 1928 | tf_op jit(solution)/shard_map/ppermute | solution.py:19
  27.5 1.9 collective-permute-start
  29.6 6.4 %collective-permute-done = f32[10,4,4,1]{3,2,1,0:T(4,128)S(1)} collective-permute-done((f32[10,4,4,1]{3,2,1,0:T(4,128)S(1)}, f32[10,4,4,1]{3,2,1,0:T(4,128)S(1)}, u32[]{:S(2)}, u32[]{:S(2)}) %collective-permute-start) | collective-permute-done | bytes 672 | tf_op jit(solution)/shard_map/ppermute | solution.py:16
  36.4 1.3 collective-permute-start.2
  37.7 4.5 %collective-permute-start.3 = (f32[10,4,1,258]{3,2,1,0:T(1,128)S(1)}, f32[10,4,1,258]{3,2,1,0:T(1,128)S(1)}, u32[]{:S(2)}, u32[]{:S(2)}) collective-permute-start(f32[10,4,1,258]{3,2,1,0:T(1,128)S(1)} %get-tuple-element.21), channel_id=1, source_target_pairs={{4,0},{8,4},{12,8},{5,1},{9,5},{13,9},{6,2},{10,6},{14,10},{7,3},{... | collective-permute-start | bytes 123848 | tf_op jit(solution)/shard_map/ppermute | solution.py:19
  42.5 1.6 collective-permute-done.3
  44.3 1.3 collective-permute-start.5
  45.6 3.0 collective-permute-start.4
  51.1 1.9 collective-permute-start.7
  53.0 3.9 %collective-permute-start.6 = (f32[8,4,4,1]{3,2,1,0:T(4,128)S(1)}, f32[8,4,4,1]{3,2,1,0:T(4,128)S(1)}, u32[]{:S(2)}, u32[]{:S(2)}) collective-permute-start(f32[8,4,4,1]{3,2,1,0:T(4,128)S(1)} %get-tuple-element.31), channel_id=1, source_target_pairs={{0,16},{16,32},{32,48},{48,64},{64,80},{80,96},{96,112},{112,128},... | collective-permute-start | bytes 1544 | tf_op jit(solution)/shard_map/ppermute | solution.py:16
  57.8 3.9 %collective-permute-done.6 = f32[8,4,4,1]{3,2,1,0:T(4,128)S(1)} collective-permute-done((f32[8,4,4,1]{3,2,1,0:T(4,128)S(1)}, f32[8,4,4,1]{3,2,1,0:T(4,128)S(1)}, u32[]{:S(2)}, u32[]{:S(2)}) %collective-permute-start.6) | collective-permute-done | bytes 544 | tf_op jit(solution)/shard_map/ppermute | solution.py:16
  62.0 4.2 %collective-permute-start.9 = (f32[8,4,1,258]{3,2,1,0:T(1,128)S(1)}, f32[8,4,1,258]{3,2,1,0:T(1,128)S(1)}, u32[]{:S(2)}, u32[]{:S(2)}) collective-permute-start(f32[8,4,1,258]{3,2,1,0:T(1,128)S(1)} %get-tuple-element.26), channel_id=1, source_target_pairs={{4,0},{8,4},{12,8},{5,1},{9,5},{13,9},{6,2},{10,6},{14,10},{7,3},{... | collective-permute-start | bytes 99080 | tf_op jit(solution)/shard_map/ppermute | solution.py:19
  66.2 1.3 collective-permute-start.8
  67.9 4.3 %collective-permute-done.8 = f32[8,4,1,258]{3,2,1,0:T(1,128)S(1)} collective-permute-done((f32[8,4,1,258]{3,2,1,0:T(1,128)S(1)}, f32[8,4,1,258]{3,2,1,0:T(1,128)S(1)}, u32[]{:S(2)}, u32[]{:S(2)}) %collective-permute-start.8) | collective-permute-done | bytes 33056 | tf_op jit(solution)/shard_map/ppermute | solution.py:16
  72.3 8.3 %collective-permute-start.10 = (f32[8,1,6,258]{3,2,1,0:T(8,128)S(1)}, f32[8,1,6,258]{3,2,1,0:T(8,128)S(1)}, u32[]{:S(2)}, u32[]{:S(2)}) collective-permute-start(f32[8,1,6,258]{3,2,1,0:T(8,128)S(1)} %get-tuple-element.20), channel_id=1, source_target_pairs={{0,1},{1,2},{2,3},{4,5},{5,6},{6,7},{8,9},{9,10},{10,11},{12,13},{... | collective-permute-start | bytes 148616 | tf_op jit(solution)/shard_map/ppermute | solution.py:16
  80.6 1.3 collective-permute-start.11
  81.9 7.3 %collective-permute-done.11 = f32[8,1,6,258]{3,2,1,0:T(8,128)S(1)} collective-permute-done((f32[8,1,6,258]{3,2,1,0:T(8,128)S(1)}, f32[8,1,6,258]{3,2,1,0:T(8,128)S(1)}, u32[]{:S(2)}, u32[]{:S(2)}) %collective-permute-start.11) | collective-permute-done | bytes 49568 | tf_op jit(solution)/shard_map/ppermute | solution.py:19
  90.7 3.2 %collective-permute-start.13 = (f32[8,4,4,1]{3,2,1,0:T(4,128)S(1)}, f32[8,4,4,1]{3,2,1,0:T(4,128)S(1)}, u32[]{:S(2)}, u32[]{:S(2)}) collective-permute-start(f32[8,4,4,1]{3,2,1,0:T(4,128)S(1)} %get-tuple-element.30), channel_id=1, source_target_pairs={{16,0},{32,16},{48,32},{64,48},{80,64},{96,80},{112,96},{128,112},... | collective-permute-start | bytes 1544 | tf_op jit(solution)/shard_map/ppermute | solution.py:19
  93.9 2.7 collective-permute-start.12
  96.5 3.1 collective-permute-done.13
  99.6 2.9 collective-permute-done.12
  102.9 3.5 %collective-permute-start.15 = (f32[8,4,1,258]{3,2,1,0:T(1,128)S(1)}, f32[8,4,1,258]{3,2,1,0:T(1,128)S(1)}, u32[]{:S(2)}, u32[]{:S(2)}) collective-permute-start(f32[8,4,1,258]{3,2,1,0:T(1,128)S(1)} %get-tuple-element.24), channel_id=1, source_target_pairs={{4,0},{8,4},{12,8},{5,1},{9,5},{13,9},{6,2},{10,6},{14,10},{7,3},{... | collective-permute-start | bytes 99080 | tf_op jit(solution)/shard_map/ppermute | solution.py:19
  106.4 1.3 collective-permute-start.14
  108.1 4.3 %collective-permute-done.14 = f32[8,4,1,258]{3,2,1,0:T(1,128)S(1)} collective-permute-done((f32[8,4,1,258]{3,2,1,0:T(1,128)S(1)}, f32[8,4,1,258]{3,2,1,0:T(1,128)S(1)}, u32[]{:S(2)}, u32[]{:S(2)}) %collective-permute-start.14) | collective-permute-done | bytes 33056 | tf_op jit(solution)/shard_map/ppermute | solution.py:16
  112.5 8.5 %collective-permute-start.16 = (f32[8,1,6,258]{3,2,1,0:T(8,128)S(1)}, f32[8,1,6,258]{3,2,1,0:T(8,128)S(1)}, u32[]{:S(2)}, u32[]{:S(2)}) collective-permute-start(f32[8,1,6,258]{3,2,1,0:T(8,128)S(1)} %get-tuple-element.18), channel_id=1, source_target_pairs={{0,1},{1,2},{2,3},{4,5},{5,6},{6,7},{8,9},{9,10},{10,11},{12,13},{... | collective-permute-start | bytes 148616 | tf_op jit(solution)/shard_map/ppermute | solution.py:16
  121.0 1.3 collective-permute-start.17
  122.3 1.3 dynamic-slice
  125.2 182.7 %all-reduce.3.cloned.1.call-done = f32[128,8192]{1,0:T(8,128)} async-done(((f32[128,8192]{1,0:T(8,128)}), f32[128,8192]{1,0:T(8,128)}) %all-reduce.3.cloned.1.call-update) | async-done | bytes 4194320
  308.9 1.7 fusion.20
  (52 shorter events, 10.9 us)
Async XLA Ops:
  6.5 301.4 %all-reduce.3.cloned.1.call-start = ((), (), s32[]{:S(2)}) async-start(), calls=%async_computation | async-start | bytes 8388608
  8.6 3.6 %copy-start.5 = (s32[64]{0:T(128)S(1)}, s32[64]{0:T(128)}, u32[]{:S(2)}) copy-start(s32[64]{0:T(128)} %param.18) | copy-start | bytes 772
  8.6 3.6 %copy-start.6 = (s32[64,1]{0,1:T(1,128)S(1)}, s32[64,1]{0,1:T(1,128)}, u32[]{:S(2)}) copy-start(s32[64,1]{0,1:T(1,128)} %param.17) | copy-start | bytes 772
  12.2 2.8 copy-start
  12.2 2.8 copy-start.1
  12.2 2.8 copy-start.2
  14.9 33.7 %copy-start.4 = (f32[16]{0:T(128)S(1)}, f32[16]{0:T(128)}, u32[]{:S(2)}) copy-start(f32[16]{0:T(128)} %param.14) | copy-start | bytes 196
  14.9 35.1 %copy-start.3 = (f32[8]{0:T(128)S(1)}, f32[8]{0:T(128)}, u32[]{:S(2)}) copy-start(f32[8]{0:T(128)} %param.13) | copy-start | bytes 100
  15.1 14.5 %collective-permute-start.1 = (f32[10,4,4,1]{3,2,1,0:T(4,128)S(1)}, f32[10,4,4,1]{3,2,1,0:T(4,128)S(1)}, u32[]{:S(2)}, u32[]{:S(2)}) collective-permute-start(f32[10,4,4,1]{3,2,1,0:T(4,128)S(1)} %get-tuple-element.28), channel_id=1, source_target_pairs={{16,0},{32,16},{48,32},{64,48},{80,64},{96,80},{112,96},{128,112},... | collective-permute-start | bytes 1928 | tf_op jit(solution)/shard_map/ppermute | solution.py:19
  27.5 8.4 %collective-permute-start = (f32[10,4,4,1]{3,2,1,0:T(4,128)S(1)}, f32[10,4,4,1]{3,2,1,0:T(4,128)S(1)}, u32[]{:S(2)}, u32[]{:S(2)}) collective-permute-start(f32[10,4,4,1]{3,2,1,0:T(4,128)S(1)} %get-tuple-element.27), channel_id=1, source_target_pairs={{0,16},{16,32},{32,48},{48,64},{64,80},{80,96},{96,112},{112,128},... | collective-permute-start | bytes 1928 | tf_op jit(solution)/shard_map/ppermute | solution.py:16
  36.4 6.1 %collective-permute-start.2 = (f32[10,4,1,258]{3,2,1,0:T(1,128)S(1)}, f32[10,4,1,258]{3,2,1,0:T(1,128)S(1)}, u32[]{:S(2)}, u32[]{:S(2)}) collective-permute-start(f32[10,4,1,258]{3,2,1,0:T(1,128)S(1)} %get-tuple-element.22), channel_id=1, source_target_pairs={{0,4},{4,8},{8,12},{1,5},{5,9},{9,13},{2,6},{6,10},{10,14},{3,7},{... | collective-permute-start | bytes 123848 | tf_op jit(solution)/shard_map/ppermute | solution.py:16
  37.7 6.4 %collective-permute-start.3 = (f32[10,4,1,258]{3,2,1,0:T(1,128)S(1)}, f32[10,4,1,258]{3,2,1,0:T(1,128)S(1)}, u32[]{:S(2)}, u32[]{:S(2)}) collective-permute-start(f32[10,4,1,258]{3,2,1,0:T(1,128)S(1)} %get-tuple-element.21), channel_id=1, source_target_pairs={{4,0},{8,4},{12,8},{5,1},{9,5},{13,9},{6,2},{10,6},{14,10},{7,3},{... | collective-permute-start | bytes 123848 | tf_op jit(solution)/shard_map/ppermute | solution.py:19
  44.3 4.6 %collective-permute-start.5 = (f32[10,1,6,258]{3,2,1,0:T(8,128)S(1)}, f32[10,1,6,258]{3,2,1,0:T(8,128)S(1)}, u32[]{:S(2)}, u32[]{:S(2)}) collective-permute-start(f32[10,1,6,258]{3,2,1,0:T(8,128)S(1)} %get-tuple-element.16), channel_id=1, source_target_pairs={{1,0},{2,1},{3,2},{5,4},{6,5},{7,6},{9,8},{10,9},{11,10},{13,12},{... | collective-permute-start | bytes 185768 | tf_op jit(solution)/shard_map/ppermute | solution.py:19
  45.6 4.0 %collective-permute-start.4 = (f32[10,1,6,258]{3,2,1,0:T(8,128)S(1)}, f32[10,1,6,258]{3,2,1,0:T(8,128)S(1)}, u32[]{:S(2)}, u32[]{:S(2)}) collective-permute-start(f32[10,1,6,258]{3,2,1,0:T(8,128)S(1)} %get-tuple-element.15), channel_id=1, source_target_pairs={{0,1},{1,2},{2,3},{4,5},{5,6},{6,7},{8,9},{9,10},{10,11},{12,13},{... | collective-permute-start | bytes 185768 | tf_op jit(solution)/shard_map/ppermute | solution.py:16
  51.1 6.7 %collective-permute-start.7 = (f32[8,4,4,1]{3,2,1,0:T(4,128)S(1)}, f32[8,4,4,1]{3,2,1,0:T(4,128)S(1)}, u32[]{:S(2)}, u32[]{:S(2)}) collective-permute-start(f32[8,4,4,1]{3,2,1,0:T(4,128)S(1)} %get-tuple-element.32), channel_id=1, source_target_pairs={{16,0},{32,16},{48,32},{64,48},{80,64},{96,80},{112,96},{128,112},... | collective-permute-start | bytes 1544 | tf_op jit(solution)/shard_map/ppermute | solution.py:19
  53.0 8.6 %collective-permute-start.6 = (f32[8,4,4,1]{3,2,1,0:T(4,128)S(1)}, f32[8,4,4,1]{3,2,1,0:T(4,128)S(1)}, u32[]{:S(2)}, u32[]{:S(2)}) collective-permute-start(f32[8,4,4,1]{3,2,1,0:T(4,128)S(1)} %get-tuple-element.31), channel_id=1, source_target_pairs={{0,16},{16,32},{32,48},{48,64},{64,80},{80,96},{96,112},{112,128},... | collective-permute-start | bytes 1544 | tf_op jit(solution)/shard_map/ppermute | solution.py:16
  62.0 5.9 %collective-permute-start.9 = (f32[8,4,1,258]{3,2,1,0:T(1,128)S(1)}, f32[8,4,1,258]{3,2,1,0:T(1,128)S(1)}, u32[]{:S(2)}, u32[]{:S(2)}) collective-permute-start(f32[8,4,1,258]{3,2,1,0:T(1,128)S(1)} %get-tuple-element.26), channel_id=1, source_target_pairs={{4,0},{8,4},{12,8},{5,1},{9,5},{13,9},{6,2},{10,6},{14,10},{7,3},{... | collective-permute-start | bytes 99080 | tf_op jit(solution)/shard_map/ppermute | solution.py:19
  66.2 6.0 %collective-permute-start.8 = (f32[8,4,1,258]{3,2,1,0:T(1,128)S(1)}, f32[8,4,1,258]{3,2,1,0:T(1,128)S(1)}, u32[]{:S(2)}, u32[]{:S(2)}) collective-permute-start(f32[8,4,1,258]{3,2,1,0:T(1,128)S(1)} %get-tuple-element.25), channel_id=1, source_target_pairs={{0,4},{4,8},{8,12},{1,5},{5,9},{9,13},{2,6},{6,10},{10,14},{3,7},{... | collective-permute-start | bytes 99080 | tf_op jit(solution)/shard_map/ppermute | solution.py:16
  72.3 9.6 %collective-permute-start.10 = (f32[8,1,6,258]{3,2,1,0:T(8,128)S(1)}, f32[8,1,6,258]{3,2,1,0:T(8,128)S(1)}, u32[]{:S(2)}, u32[]{:S(2)}) collective-permute-start(f32[8,1,6,258]{3,2,1,0:T(8,128)S(1)} %get-tuple-element.20), channel_id=1, source_target_pairs={{0,1},{1,2},{2,3},{4,5},{5,6},{6,7},{8,9},{9,10},{10,11},{12,13},{... | collective-permute-start | bytes 148616 | tf_op jit(solution)/shard_map/ppermute | solution.py:16
  80.6 8.7 %collective-permute-start.11 = (f32[8,1,6,258]{3,2,1,0:T(8,128)S(1)}, f32[8,1,6,258]{3,2,1,0:T(8,128)S(1)}, u32[]{:S(2)}, u32[]{:S(2)}) collective-permute-start(f32[8,1,6,258]{3,2,1,0:T(8,128)S(1)} %get-tuple-element.19), channel_id=1, source_target_pairs={{1,0},{2,1},{3,2},{5,4},{6,5},{7,6},{9,8},{10,9},{11,10},{13,12},{... | collective-permute-start | bytes 148616 | tf_op jit(solution)/shard_map/ppermute | solution.py:19
  90.7 8.9 %collective-permute-start.13 = (f32[8,4,4,1]{3,2,1,0:T(4,128)S(1)}, f32[8,4,4,1]{3,2,1,0:T(4,128)S(1)}, u32[]{:S(2)}, u32[]{:S(2)}) collective-permute-start(f32[8,4,4,1]{3,2,1,0:T(4,128)S(1)} %get-tuple-element.30), channel_id=1, source_target_pairs={{16,0},{32,16},{48,32},{64,48},{80,64},{96,80},{112,96},{128,112},... | collective-permute-start | bytes 1544 | tf_op jit(solution)/shard_map/ppermute | solution.py:19
  93.9 8.7 %collective-permute-start.12 = (f32[8,4,4,1]{3,2,1,0:T(4,128)S(1)}, f32[8,4,4,1]{3,2,1,0:T(4,128)S(1)}, u32[]{:S(2)}, u32[]{:S(2)}) collective-permute-start(f32[8,4,4,1]{3,2,1,0:T(4,128)S(1)} %get-tuple-element.29), channel_id=1, source_target_pairs={{0,16},{16,32},{32,48},{48,64},{64,80},{80,96},{96,112},{112,128},... | collective-permute-start | bytes 1544 | tf_op jit(solution)/shard_map/ppermute | solution.py:16
  102.9 5.3 %collective-permute-start.15 = (f32[8,4,1,258]{3,2,1,0:T(1,128)S(1)}, f32[8,4,1,258]{3,2,1,0:T(1,128)S(1)}, u32[]{:S(2)}, u32[]{:S(2)}) collective-permute-start(f32[8,4,1,258]{3,2,1,0:T(1,128)S(1)} %get-tuple-element.24), channel_id=1, source_target_pairs={{4,0},{8,4},{12,8},{5,1},{9,5},{13,9},{6,2},{10,6},{14,10},{7,3},{... | collective-permute-start | bytes 99080 | tf_op jit(solution)/shard_map/ppermute | solution.py:19
  106.4 6.0 %collective-permute-start.14 = (f32[8,4,1,258]{3,2,1,0:T(1,128)S(1)}, f32[8,4,1,258]{3,2,1,0:T(1,128)S(1)}, u32[]{:S(2)}, u32[]{:S(2)}) collective-permute-start(f32[8,4,1,258]{3,2,1,0:T(1,128)S(1)} %get-tuple-element.23), channel_id=1, source_target_pairs={{0,4},{4,8},{8,12},{1,5},{5,9},{9,13},{2,6},{6,10},{10,14},{3,7},{... | collective-permute-start | bytes 99080 | tf_op jit(solution)/shard_map/ppermute | solution.py:16
  112.5 11.7 %collective-permute-start.16 = (f32[8,1,6,258]{3,2,1,0:T(8,128)S(1)}, f32[8,1,6,258]{3,2,1,0:T(8,128)S(1)}, u32[]{:S(2)}, u32[]{:S(2)}) collective-permute-start(f32[8,1,6,258]{3,2,1,0:T(8,128)S(1)} %get-tuple-element.18), channel_id=1, source_target_pairs={{0,1},{1,2},{2,3},{4,5},{5,6},{6,7},{8,9},{9,10},{10,11},{12,13},{... | collective-permute-start | bytes 148616 | tf_op jit(solution)/shard_map/ppermute | solution.py:16
  121.0 3.9 %collective-permute-start.17 = (f32[8,1,6,258]{3,2,1,0:T(8,128)S(1)}, f32[8,1,6,258]{3,2,1,0:T(8,128)S(1)}, u32[]{:S(2)}, u32[]{:S(2)}) collective-permute-start(f32[8,1,6,258]{3,2,1,0:T(8,128)S(1)} %get-tuple-element.17), channel_id=1, source_target_pairs={{1,0},{2,1},{3,2},{5,4},{6,5},{7,6},{9,8},{10,9},{11,10},{13,12},{... | collective-permute-start | bytes 148616 | tf_op jit(solution)/shard_map/ppermute | solution.py:19
Sparse Core Ops, SparseCore 0:
  15.0 292.8 all-reduce.2
where the time goes:
time: 318 us; the launch traced here: 317 us
  waiting for transfers between devices  220 us (69%)
  starting transfers between devices  65.8 us (21%)
  between operations  14.5 us (5%)
  other arithmetic  8.52 us (3%)
  matrix products  5.59 us (2%)
  local copies, waits for them, and re-layouts  3.21 us (1%)
    unnamed x2, waiting for transfers between devices  183 us
    ppermute x9, starting transfers between devices, extended_2(): lax.ppermute(lax.slice_in_dim(block, 0, width, axis=dim), axis, backward)  33.7 us
    ppermute x9, starting transfers between devices, extended_2(): lax.ppermute(lax.slice_in_dim(block, block.shape[dim] - width, None, axis...  32.2 us
    ppermute x9, waiting for transfers between devices, extended_2(): lax.ppermute(lax.slice_in_dim(block, block.shape[dim] - width, None, axis...  22.7 us
    ppermute x9, waiting for transfers between devices, extended_2(): lax.ppermute(lax.slice_in_dim(block, 0, width, axis=dim), axis, backward)  14.4 us
  transfers between devices with their start and end apart: 19, of which 15 were waited for; matrix products, arithmetic and copies ran while one was open for 2% of the time, Pallas kernels for 0%

commit v1 on v0

v1 whole, which is shorter than its diff:
```python
import functools

import jax
import jax.numpy as jnp
from jax import lax
from jax.experimental import pallas as pl
from jax.experimental.pallas import tpu as pltpu
from jax.sharding import PartitionSpec as P

STEPS = 3
CAP = 4
SPLIT = 80
TOP = 32000.0
MESH = pl.DeviceIdType.MESH
F32 = jnp.float32


def encode(x):
    rows = x.shape[0]
    peak = jnp.max(jnp.abs(x).reshape(rows // 8, 8, 256), axis=0)
    peak = jnp.maximum(peak[:, :128], peak[:, 128:])
    peak = jnp.maximum(jnp.max(peak, axis=0, keepdims=True), 1e-30)
    gain = TOP / peak
    gain = jnp.concatenate([gain, gain], axis=1)
    return jnp.round(x * gain).astype(jnp.int32).astype(jnp.int16), peak * (1.0 / TOP)


def decode(ints, scale):
    scale = jnp.concatenate([scale, scale], axis=1)
    return ints.astype(jnp.int32).astype(F32) * scale


def kernel(
    sizes,
    vd_s,
    hd_s,
    row_s,
    adj_ref,
    cu_ref,
    cv_ref,
    inn_ref,
    own_ref,
    op_hbm,
    out_ref,
    ops,
    op_sem,
    prod,
    code_v,
    code_s,
    code_sem,
    mine,
    other,
    ysend,
    yrecv,
    y_sems,
    asend,
    arecv,
    bsend,
    brecv,
    scale_send,
    scale_recv,
    ring_send_sem,
    ring_recv_sem,
    scale_send_sem,
    scale_recv_sem,
    fsend,
    frecv,
    fscale_send,
    fscale_recv,
    f_sems,
    fields,
    lev_lo,
    lev_hi,
    lat_lo,
    lat_hi,
    wind_send,
    wind_recv,
    lon_send,
    lon_recv,
    halo_send_sem,
    halo_recv_sem,
    wind_sems,
):
    n_lon, n_lat, n_lev = sizes
    nz = n_lon // 2
    half = nz // 2
    nb = prod.shape[0] - 1
    lon, lat, lev = (lax.axis_index(name) for name in ("lon", "lat", "lev"))
    z, yl = lon // 2, lon % 2
    partner = z * 2 + (1 - yl)
    ring = (((z + 1) % nz) * 2 + yl, ((z + nz - 1) % nz) * 2 + yl)
    east, west = (lon + 1) % n_lon, (lon + n_lon - 1) % n_lon

    groups = op_sem.shape[0]
    per = nb // groups

    def fetch(g):
        return pltpu.make_async_copy(
            op_hbm.at[pl.ds(g * per, per)], ops.at[pl.ds(g * per, per)], op_sem.at[g]
        )

    for g in range(groups):
        fetch(g).start()

    barrier = pltpu.get_barrier_semaphore()
    greet = [{"lon": t} for t in (ring[0], ring[1], east, west)]
    greet += [{"lat": (lat + 1) % n_lat}, {"lat": (lat + n_lat - 1) % n_lat}]
    greet += [{"lev": (lev + 1) % n_lev}, {"lev": (lev + n_lev - 1) % n_lev}]
    for target in greet:
        pl.semaphore_signal(barrier, inc=1, device_id=target, device_id_type=MESH)

    bi = lax.broadcasted_iota(jnp.int32, (nb, nb), 0)
    bj = lax.broadcasted_iota(jnp.int32, (nb, nb), 1)
    tcol = own_ref[...]
    trow = jnp.sum(jnp.where(bi == bj, tcol, 0), axis=0, keepdims=True)
    earlier = jnp.where((tcol == trow) & (bj < bi), 1.0, 0.0)
    place = jnp.sum(earlier, axis=1, keepdims=True).astype(jnp.int32)
    slot = lax.broadcasted_iota(jnp.int32, (nb, 128), 1)
    number = lax.broadcasted_iota(jnp.int32, (nb, 128), 0)
    hit = (tcol == slot // CAP) & (place == slot % CAP)
    code_v[...] = jnp.sum(jnp.where(hit, number - nb, 0), axis=0, keepdims=True) + nb
    to_smem = pltpu.make_async_copy(code_v, code_s, code_sem)
    to_smem.start()

    for j in range(4):
        for k in range(4):
            fields[0, j, k] = adj_ref[:, k, j, :]
    u_first = jnp.concatenate(
        [
            jnp.broadcast_to(cu_ref[k, pl.ds(j, 1), 0:128], (8, 128))
            for j in range(4)
            for k in range(4)
        ],
        axis=0,
    ).T[0:1]
    wind_send[...] = jnp.zeros_like(wind_send)
    for k in range(4):
        wind_send[pl.ds(k, 1)] = cv_ref[k, pl.ds(0, 1), :]
    at_south, at_north = lat == 0, lat == n_lat - 1
    at_low, at_high = lev == 0, lev == n_lev - 1

    @pl.when(at_south)
    def _():
        lat_lo[...] = jnp.zeros_like(lat_lo)

    @pl.when(at_north)
    def _():
        lat_hi[...] = jnp.zeros_like(lat_hi)
        wind_recv[...] = jnp.zeros_like(wind_recv)

    @pl.when(at_low)
    def _():
        lev_lo[...] = jnp.zeros_like(lev_lo)

    @pl.when(at_high)
    def _():
        lev_hi[...] = jnp.zeros_like(lev_hi)

    prod[nb] = jnp.zeros_like(prod[nb])

    def multiply(g, carry):
        fetch(g).wait()
        for i in range(per):
            b = g * per + i
            p = jnp.dot(inn_ref[b], ops[b], preferred_element_type=F32)
            prod[b] = p.astype(jnp.bfloat16).astype(F32)
        return carry

    lax.fori_loop(0, groups, multiply, 0)

    pl.semaphore_wait(barrier, len(greet))

    def halo(r):
        def copy(q, src, dst, target):
            return pltpu.make_async_remote_copy(
                src_ref=src,
                dst_ref=dst,
                send_sem=halo_send_sem.at[q, r],
                recv_sem=halo_recv_sem.at[q, r],
                device_id=target,
                device_id_type=MESH,
            )

        return (
            copy(0, fields.at[r, 3], lat_lo.at[r], {"lat": (lat + 1) % n_lat}),
            copy(1, fields.at[r, 0], lat_hi.at[r], {"lat": (lat + n_lat - 1) % n_lat}),
            copy(2, fields.at[r, :, 3], lev_lo.at[r], {"lev": (lev + 1) % n_lev}),
            copy(3, fields.at[r, :, 0], lev_hi.at[r], {"lev": (lev + n_lev - 1) % n_lev}),
            copy(4, lon_send.at[r, 0], lon_recv.at[r, 0], {"lon": east}),
            copy(5, lon_send.at[r, 1], lon_recv.at[r, 1], {"lon": west}),
        )

    wind = pltpu.make_async_remote_copy(
        src_ref=wind_send,
        dst_ref=wind_recv,
        send_sem=wind_sems.at[0],
        recv_sem=wind_sems.at[1],
        device_id={"lat": (lat + n_lat - 1) % n_lat},
        device_id_type=MESH,
    )
    sends = (~at_north, ~at_south, ~at_high, ~at_low, None, None)
    arrives = (~at_south, ~at_north, ~at_low, ~at_high, None, None)

    def gated(flag, action):
        if flag is None:
            action()
        else:
            pl.when(flag)(action)

    def send_halo(r):
        flat = fields[r].reshape(128, 256)
        first = flat[:, 0:128].T[0:1]
        last = flat[:, 128:256].T[127:128]
        lon_send[r, 0, pl.ds(0, 1)] = last
        lon_send[r, 1, pl.ds(0, 1)] = first
        lon_send[r, 1, pl.ds(1, 1)] = first * u_first
        for flag, copy in zip(sends, halo(r)):
            gated(flag, copy.start)

    lon_send[...] = jnp.zeros_like(lon_send)
    send_halo(0)
    gated(sends[1], wind.start)

    lane = lax.broadcasted_iota(jnp.int32, (8, 256), 1)
    field = lax.broadcasted_iota(jnp.int32, (8, 256), 0)
    gain = jnp.zeros((8, 256), F32)
    for f in range(8):
        gain = jnp.where(field == f, hd_s[f], gain)

    def sub_step(r):
        for flag, copy in zip(arrives, halo(r)):
            gated(flag, copy.wait_recv)
        edges = jnp.concatenate([lon_recv[r, 0], lon_recv[r, 1]], axis=0).T

        def at(j, k):
            if j < 0:
                return lat_lo[r, k]
            if j > 3:
                return lat_hi[r, k]
            if k < 0:
                return lev_lo[r, j]
            if k > 3:
                return lev_hi[r, j]
            return fields[r, j, k]

        def north_wind(j, k):
            return wind_recv[pl.ds(k, 1)] if j > 3 else cv_ref[k, pl.ds(j, 1), :]

        for k in range(4):
            level = lev * 4 + k
            up = jnp.where(level < n_lev * 4 - 1, vd_s[level], 0.0)
            down = jnp.where(level > 0, vd_s[jnp.maximum(level - 1, 0)], 0.0)
            for j in range(4):
                a = at(j, k)
                rows = slice((j * 4 + k) * 8, (j * 4 + k) * 8 + 8)
                flux = cu_ref[k, pl.ds(j, 1), :] * a
                north_flux = cv_ref[k, pl.ds(j, 1), :] * a
                north, south = at(j + 1, k), at(j - 1, k)
                a_east = jnp.where(lane == 255, edges[rows, 8:9], pltpu.roll(a, 255, 1))
                a_west = jnp.where(lane == 0, edges[rows, 0:1], pltpu.roll(a, 1, 1))
                moved = jnp.where(lane == 255, edges[rows, 9:10], pltpu.roll(flux, 255, 1))
                res = a - flux - north_flux + moved + north_wind(j + 1, k) * north
                res = res + gain * (a_east + a_west + north + south - 4.0 * a)
                res = res + up * (at(j, k + 1) - a)
                res = res + down * (at(j, k - 1) - a)
                fields[r + 1, j, k] = res

    def full_step(r):
        if isinstance(r, int):
            if r == 0:
                gated(arrives[1], wind.wait_recv)
        else:
            pl.when((r == 0) & ~at_north)(wind.wait_recv)
        sub_step(r)
        if isinstance(r, int):
            if r < STEPS - 1:
                send_halo(r + 1)
        else:
            pl.when(r < STEPS - 1)(lambda: send_halo(r + 1))

    to_smem.wait()

    def tile_sum(tile):
        total = [jnp.zeros((32, 256), F32) for j in range(4)]
        for c in range(CAP):
            b = code_s[0, tile * CAP + c]
            row = row_s[jnp.minimum(b, nb - 1)]
            p = prod[b]
            for j in range(4):
                total[j] = total[j] + p * jnp.where(row == j, 1.0, 0.0)
        return jnp.concatenate(total, axis=0)

    def ycopy(n):
        return pltpu.make_async_remote_copy(
            src_ref=ysend.at[n],
            dst_ref=yrecv.at[n],
            send_sem=y_sems.at[0, n],
            recv_sem=y_sems.at[1, n],
            device_id={"lon": partner},
            device_id_type=MESH,
        )

    def gather(n, carry):
        away = half - (n + 1) // 2
        dest = (z + nz + away * (2 * (n % 2) - 1)) % nz
        theirs = tile_sum(dest * 2 + (1 - yl))
        ysend[n] = theirs[:SPLIT].astype(jnp.bfloat16)
        ycopy(n).start()
        other[n] = theirs[SPLIT:]
        mine[n] = tile_sum(dest * 2 + yl)
        return carry

    def ring_copy(part, way, s):
        src, dst = ((asend, arecv), (bsend, brecv))[part]
        q = part * 2 + way
        data = pltpu.make_async_remote_copy(
            src_ref=src.at[way, s],
            dst_ref=dst.at[way, s],
            send_sem=ring_send_sem.at[q, s],
            recv_sem=ring_recv_sem.at[q, s],
            device_id={"lon": ring[way]},
            device_id_type=MESH,
        )
        scale = pltpu.make_async_remote_copy(
            src_ref=scale_send.at[q, s],
            dst_ref=scale_recv.at[q, s],
            send_sem=scale_send_sem.at[q, s],
            recv_sem=scale_recv_sem.at[q, s],
            device_id={"lon": ring[way]},
            device_id_type=MESH,
        )
        return data, scale

    def own_part(part, n):
        if part == 0:
            ycopy(n).wait_recv()
            return mine[n, :SPLIT] + yrecv[n].astype(F32)
        return jnp.concatenate([mine[n, SPLIT:], other[n]], axis=0)

    def arrived(part, way, s):
        for copy in ring_copy(part, way, s):
            copy.wait_recv()
        buf = (arecv, brecv)[part]
        return decode(buf[way, s], scale_recv[part * 2 + way, s])

    def ring_step(part, way, s, first):
        n = 2 * s - 1 + way
        if isinstance(s, int):
            n = max(n, 0)
        x = own_part(part, n)
        if not first:
            x = x + arrived(part, way, s - 1)
        ints, scale = encode(x)
        (asend, bsend)[part][way, s] = ints
        scale_send[part * 2 + way, s] = scale
        for copy in ring_copy(part, way, s):
            copy.start()

    def gather_range(lo, hi):
        lax.fori_loop(lo, hi, gather, 0)

    gather_range(0, min(5, nz))
    ring_step(1, 1, 0, True)
    ring_step(0, 0, 0, True)
    gather_range(min(5, nz), min(7, nz))
    ring_step(1, 1, 1, False)
    ring_step(1, 0, 1, True)
    ring_step(0, 0, 1, False)
    ring_step(0, 1, 1, True)
    gather_range(min(7, nz), min(9, nz))

    def later(s, carry):
        for part in (1, 0):
            for way in (0, 1):
                ring_step(part, way, s, False)
        lax.fori_loop(jnp.minimum(2 * s + 5, nz), jnp.minimum(2 * s + 7, nz), gather, 0)

        @pl.when((s % 2 == 0) & (s <= 2 * STEPS))
        def _():
            full_step(s // 2 - 1)

        return carry

    lax.fori_loop(2, half, later, 0)
    for r in range(sum(1 for s in range(2, half) if s % 2 == 0 and s <= 2 * STEPS), STEPS):
        full_step(r)

    last = half - 1
    line = own_part(1, nz - 1) + arrived(1, 0, last) + arrived(1, 1, last)
    rest = 128 - SPLIT
    ints, scale = encode(line[rest:])
    fsend[...] = ints
    fscale_send[...] = scale
    finals = [
        pltpu.make_async_remote_copy(
            src_ref=src,
            dst_ref=dst,
            send_sem=f_sems.at[q, 0],
            recv_sem=f_sems.at[q, 1],
            device_id={"lon": partner},
            device_id_type=MESH,
        )
        for q, (src, dst) in enumerate(((fsend, frecv), (fscale_send, fscale_recv)))
    ]
    for copy in finals:
        copy.start()
    result = fields[STEPS].reshape(128, 256)
    total = own_part(0, nz - 1) + arrived(0, 0, last) + arrived(0, 1, last)
    out_ref[:SPLIT] = result[:SPLIT] + total
    for copy in finals:
        copy.wait_recv()
    out_ref[SPLIT:] = result[SPLIT:] + line[:rest] + decode(frecv[...], fscale_recv[...])

    for copy in finals:
        copy.wait_send()

    def y_left(n, carry):
        ycopy(n).wait_send()
        return carry

    lax.fori_loop(0, nz, y_left, 0)

    def ring_left(s, carry):
        for part in range(2):
            for way in range(2):
                for copy in ring_copy(part, way, s):
                    copy.wait_send()
        return carry

    lax.fori_loop(1, half, ring_left, 0)
    for part in range(2):
        for copy in ring_copy(part, part, 0):
            copy.wait_send()
    gated(sends[1], wind.wait_send)

    def halo_left(r, carry):
        for flag, copy in zip(sends, halo(r)):
            gated(flag, copy.wait_send)
        return carry

    lax.fori_loop(0, STEPS, halo_left, 0)


def on_device(
    adjoint_in,
    courant_lon,
    courant_lat,
    horiz_diff,
    vert_diff,
    innovations,
    obs_operator,
    owner_tile,
    block_row,
    obs_count,
):
    nb, _, _, obs = innovations.shape
    sizes = tuple(lax.axis_size(name) for name in ("lon", "lat", "lev"))
    nz = sizes[0] // 2
    half = nz // 2
    rest = 128 - SPLIT
    observed = jnp.arange(obs, dtype=jnp.int32)[None, :] < obs_count[:, None]
    masked = jnp.where(observed[:, None, None, :], innovations, jnp.zeros((), jnp.bfloat16))
    masked = masked.transpose(0, 2, 1, 3).reshape(nb, 32, obs)

    vmem = pl.BlockSpec(memory_space=pltpu.VMEM)
    smem = pl.BlockSpec(memory_space=pltpu.SMEM)
    hbm = pl.BlockSpec(memory_space=pl.ANY)
    dma = pltpu.SemaphoreType.DMA
    i16, bf16, f32 = jnp.int16, jnp.bfloat16, jnp.float32
    out = pl.pallas_call(
        functools.partial(kernel, sizes),
        out_shape=jax.ShapeDtypeStruct((128, 256), f32),
        in_specs=[smem, smem, smem, vmem, vmem, vmem, vmem, vmem, hbm],
        out_specs=vmem,
        scratch_shapes=[
            pltpu.VMEM(obs_operator.shape, bf16),
            dma((8,)),
            pltpu.VMEM((nb + 1, 32, 256), f32),
            pltpu.VMEM((1, 128), jnp.int32),
            pltpu.SMEM((1, 128), jnp.int32),
            dma,
            pltpu.VMEM((nz, 128, 256), f32),
            pltpu.VMEM((nz, rest, 256), f32),
            pltpu.VMEM((nz, SPLIT, 256), bf16),
            pltpu.VMEM((nz, SPLIT, 256), bf16),
            dma((2, nz)),
            pltpu.VMEM((2, half, SPLIT, 256), i16),
            pltpu.VMEM((2, half, SPLIT, 256), i16),
            pltpu.VMEM((2, half, 2 * rest, 256), i16),
            pltpu.VMEM((2, half, 2 * rest, 256), i16),
            pltpu.VMEM((4, half, 1, 128), f32),
            pltpu.VMEM((4, half, 1, 128), f32),
            dma((4, half)),
            dma((4, half)),
            dma((4, half)),
            dma((4, half)),
            pltpu.VMEM((rest, 256), i16),
            pltpu.VMEM((rest, 256), i16),
            pltpu.VMEM((1, 128), f32),
            pltpu.VMEM((1, 128), f32),
            dma((2, 2)),
            pltpu.VMEM((STEPS + 1, 4, 4, 8, 256), f32),
            pltpu.VMEM((STEPS, 4, 8, 256), f32),
            pltpu.VMEM((STEPS, 4, 8, 256), f32),
            pltpu.VMEM((STEPS, 4, 8, 256), f32),
            pltpu.VMEM((STEPS, 4, 8, 256), f32),
            pltpu.VMEM((8, 256), f32),
            pltpu.VMEM((8, 256), f32),
            pltpu.VMEM((STEPS, 2, 8, 128), f32),
            pltpu.VMEM((STEPS, 2, 8, 128), f32),
            dma((6, STEPS)),
            dma((6, STEPS)),
            dma((2,)),
        ],
        compiler_params=pltpu.CompilerParams(
            collective_id=0, has_side_effects=True, vmem_limit_bytes=48 * 2**20
        ),
        name="adjoint",
    )(
        vert_diff,
        horiz_diff,
        block_row,
        adjoint_in,
        courant_lon,
        courant_lat,
        masked,
        owner_tile,
        obs_operator,
    )
    return out.reshape(4, 4, 8, 256).transpose(2, 1, 0, 3)


def solution(mesh):
    in_specs = (
        P(None, "lev", "lat", "lon"),
        P("lev", "lat", "lon"),
        P("lev", "lat", "lon"),
        P(),
        P(),
        P(("lon", "lat"), None, "lev", None),
        P(("lon", "lat"), None, None),
        P(("lon", "lat"), None),
        P(("lon", "lat")),
        P(("lon", "lat")),
    )
    out_specs = P(None, "lev", "lat", "lon")
    return jax.shard_map(
        on_device, mesh=mesh, in_specs=in_specs, out_specs=out_specs, check_vma=False
    )
```

time: 318 us -> 60.1 us (0.19)
  waiting for transfers between devices: 220 us -> 0 us
  starting transfers between devices: 65.8 us -> 0 us
  Pallas kernels: 0 us -> 49.7 us
  between operations: 14.5 us -> 0.03 us
  other arithmetic: 8.52 us -> 2.02 us
  matrix products: 5.59 us -> 0 us
  local copies, waits for them, and re-layouts: 3.21 us -> 8.06 us
    unnamed x2 -> x0, waiting for transfers between devices: 183 us -> none
    ppermute x18 -> x0, starting transfers between devices: 65.8 us -> none  [the longest x9 33.7 us: extended_2(): lax.ppermute(lax.slice_in_dim(block, 0, width, axis=dim), axis, backward)]
    pallas_call x0 -> x1, Pallas kernels: none -> 49.7 us  [on_device(): pl.pallas_call(functools.partial(kernel, sizes), out_shape=jax.ShapeDtype...]
    ppermute x18 -> x0, waiting for transfers between devices: 37.1 us -> none  [the longest x9 22.7 us: extended_2(): lax.ppermute(lax.slice_in_dim(block, block.shape[dim] - width, None, axis...]
    dot_general x2 -> x0, matrix products: 5.59 us -> none  [the longest x1 2.88 us: on_device(): jnp.einsum('bvo,boc->bvc', masked, obs_operator, preferred_element_type=j...]
    unnamed x17 -> x15, local copies, waits for them, and re-layouts: 2.91 us -> 7.24 us
  transfers between devices with their start and end apart: 19 -> 0, of which waited for: 15 -> 0; matrix products, arithmetic and copies ran while one was open for 2% -> 0% of each run, Pallas kernels for 0% -> 0%
where the time goes in v1:
time: 60.1 us; the launch traced here: 59.8 us
  Pallas kernels  49.7 us (83%)
  local copies, waits for them, and re-layouts  8.06 us (13%)
  other arithmetic  2.02 us (3%)
    pallas_call x1, Pallas kernels, on_device(): pl.pallas_call(functools.partial(kernel, sizes), out_shape=jax.ShapeDtype...  49.7 us
    unnamed x15, local copies, waits for them, and re-layouts  7.24 us
    transpose x1, other arithmetic, on_device(): masked = masked.transpose(0, 2, 1, 3).reshape(nb, 32, obs)  1.29 us

profile of v1, /device:TPU:6, one launch (start us, length us, event | category | flops | bytes accessed | tf_op | source)
XLA Modules:
  0.0 59.8 jit_solution(7825729293867353722)
XLA Ops:
  0.0 0.7 %iota_compare_fusion = pred[64,128]{1,0:T(8,128)(4,1)S(1)} fusion(s32[64]{0:T(128)} %param.19), kind=kLoop, calls=%fused_computation.3 | loop fusion | flops 8192 | bytes 8448 | tf_op jit(solution)/shard_map/lt | solution.py:461
  0.7 1.3 %select_bitcast_fusion = bf16[64,4,8,128]{3,1,2,0:T(4,128)(2,1)S(1)} fusion(bf16[64,8,4,128]{3,2,1,0:T(4,128)(2,1)} %param.15, pred[64,128]{1,0:T(8,128)(4,1)S(1)} %iota_compare_fusion), kind=kLoop, calls=%fused_computation.1 | loop fusion | flops 262144 | bytes 1056768 | tf_op jit(solution)/shard_map/transpose | solution.py:463
  2.0 0.1 copy.16
  2.1 0.7 %copy.12.own_ref = s32[64,1]{1,0:T(8,128)S(1)} copy(s32[64,1]{0,1:T(1,128)} %param.17) | data formatting | bytes 512 | tf_op args[7]
  2.9 0.0 copy-start
  2.9 2.2 %copy-done = bf16[64,128,256]{2,1,0:T(8,128)(2,1)S(1)} copy-done((bf16[64,128,256]{2,1,0:T(8,128)(2,1)S(1)}, bf16[64,128,256]{2,1,0:T(8,128)(2,1)}, u32[]{:S(2)}) %copy-start) | copy-done | bytes 4194328
  5.1 0.0 copy-start.1
  5.1 0.9 %copy-done.1 = f32[8,4,4,256]{3,2,1,0:T(4,128)S(1)} copy-done((f32[8,4,4,256]{3,2,1,0:T(4,128)S(1)}, f32[8,4,4,256]{3,2,1,0:T(4,128)}, u32[]{:S(2)}) %copy-start.1) | copy-done | bytes 131096
  6.0 0.0 copy-start.2
  6.0 0.7 %copy-done.2 = f32[4,4,256]{2,1,0:T(4,128)S(1)} copy-done((f32[4,4,256]{2,1,0:T(4,128)S(1)}, f32[4,4,256]{2,1,0:T(4,128)}, u32[]{:S(2)}) %copy-start.2) | copy-done | bytes 16408
  6.7 0.0 copy-start.3
  6.7 0.7 %copy-done.3 = f32[4,4,256]{2,1,0:T(4,128)S(1)} copy-done((f32[4,4,256]{2,1,0:T(4,128)S(1)}, f32[4,4,256]{2,1,0:T(4,128)}, u32[]{:S(2)}) %copy-start.3) | copy-done | bytes 16408
  7.4 0.0 copy-start.4
  7.4 0.7 %copy-done.4 = f32[16]{0:T(128)S(1)} copy-done((f32[16]{0:T(128)S(1)}, f32[16]{0:T(128)}, u32[]{:S(2)}) %copy-start.4) | copy-done | bytes 88
  8.1 0.0 copy-start.5
  8.1 0.7 %copy-done.5 = f32[8]{0:T(128)S(1)} copy-done((f32[8]{0:T(128)S(1)}, f32[8]{0:T(128)}, u32[]{:S(2)}) %copy-start.5) | copy-done | bytes 56
  8.7 0.0 copy-start.6
  8.7 0.7 %copy-done.6 = s32[64]{0:T(128)S(1)} copy-done((s32[64]{0:T(128)S(1)}, s32[64]{0:T(128)}, u32[]{:S(2)}) %copy-start.6) | copy-done | bytes 280
  9.4 49.7 %adjoint.1 = f32[128,256]{1,0:T(8,128)S(1)} custom-call(f32[16]{0:T(128)S(1)} %copy-done.4, f32[8]{0:T(128)S(1)} %copy-done.5, s32[64]{0:T(128)S(1)} %copy-done.6, f32[8,4,4,256]{3,2,1,0:T(4,128)S(1)} %copy-done.1, f32[4,4,256]{2,1,0:T(4,128)S(1)} %copy-done.2, f32[4,4,256]{2,1,0:T(4,128)S(1)} %copy-done.3, bf16[64,32,128]{2,1,0:T(8,128)(2,1)S(1)} %bitcast.9, ...), custom_call_target="tpu_custom_call" | custom-call | tf_op jit(solution)/shard_map/adjoint/pallas_call | solution.py:470
  59.0 0.7 %copy.17 = f32[4,4,8,256]{3,0,1,2:T(4,128)} copy(f32[4,4,8,256]{3,2,1,0:T(8,128)S(1)} %bitcast.10) | data formatting | bytes 262144 | tf_op jit(solution)/shard_map/reshape | solution.py:530
Async XLA Ops:
  2.9 2.2 %copy-start = (bf16[64,128,256]{2,1,0:T(8,128)(2,1)S(1)}, bf16[64,128,256]{2,1,0:T(8,128)(2,1)}, u32[]{:S(2)}) copy-start(bf16[64,128,256]{2,1,0:T(8,128)(2,1)} %op_hbm.1) | copy-start | bytes 12582916
  5.1 0.9 %copy-start.1 = (f32[8,4,4,256]{3,2,1,0:T(4,128)S(1)}, f32[8,4,4,256]{3,2,1,0:T(4,128)}, u32[]{:S(2)}) copy-start(f32[8,4,4,256]{3,2,1,0:T(4,128)} %adj_ref.1) | copy-start | bytes 393220
  6.0 0.7 %copy-start.2 = (f32[4,4,256]{2,1,0:T(4,128)S(1)}, f32[4,4,256]{2,1,0:T(4,128)}, u32[]{:S(2)}) copy-start(f32[4,4,256]{2,1,0:T(4,128)} %cu_ref.1) | copy-start | bytes 49156
  6.7 0.7 %copy-start.3 = (f32[4,4,256]{2,1,0:T(4,128)S(1)}, f32[4,4,256]{2,1,0:T(4,128)}, u32[]{:S(2)}) copy-start(f32[4,4,256]{2,1,0:T(4,128)} %cv_ref.1) | copy-start | bytes 49156
  7.4 0.7 %copy-start.4 = (f32[16]{0:T(128)S(1)}, f32[16]{0:T(128)}, u32[]{:S(2)}) copy-start(f32[16]{0:T(128)} %vd_s.1) | copy-start | bytes 196
  8.1 0.7 %copy-start.5 = (f32[8]{0:T(128)S(1)}, f32[8]{0:T(128)}, u32[]{:S(2)}) copy-start(f32[8]{0:T(128)} %hd_s.1) | copy-start | bytes 100
  8.7 0.7 %copy-start.6 = (s32[64]{0:T(128)S(1)}, s32[64]{0:T(128)}, u32[]{:S(2)}) copy-start(s32[64]{0:T(128)} %row_s.1) | copy-start | bytes 772

commit v2 on v1

--- a/solution.py
+++ b/solution.py
@@ -35,14 +35,21 @@
     vd_s,
     hd_s,
     row_s,
+    count_s,
+    own_ref,
+    adj_hbm,
+    cu_hbm,
+    cv_hbm,
+    inn_hbm,
+    op_hbm,
+    out_ref,
     adj_ref,
     cu_ref,
     cv_ref,
     inn_ref,
-    own_ref,
-    op_hbm,
-    out_ref,
     ops,
+    in_sems,
+    inn_sem,
     op_sem,
     prod,
     code_v,
@@ -80,6 +87,8 @@
     halo_send_sem,
     halo_recv_sem,
     wind_sems,
+    total_lo,
+    total_hi,
 ):
     n_lon, n_lat, n_lev = sizes
     nz = n_lon // 2
@@ -95,12 +104,21 @@
     per = nb // groups
 
     def fetch(g):
-        return pltpu.make_async_copy(
-            op_hbm.at[pl.ds(g * per, per)], ops.at[pl.ds(g * per, per)], op_sem.at[g]
+        part = pl.ds(g * per, per)
+        return (
+            pltpu.make_async_copy(inn_hbm.at[part], inn_ref.at[part], inn_sem.at[g]),
+            pltpu.make_async_copy(op_hbm.at[part], ops.at[part], op_sem.at[g]),
         )
 
+    state = [
+        pltpu.make_async_copy(src, dst, in_sems.at[q])
+        for q, (src, dst) in enumerate(((adj_hbm, adj_ref), (cu_hbm, cu_ref), (cv_hbm, cv_ref)))
+    ]
     for g in range(groups):
-        fetch(g).start()
+        for copy in fetch(g):
+            copy.start()
+    for copy in state:
+        copy.start()
 
     barrier = pltpu.get_barrier_semaphore()
     greet = [{"lon": t} for t in (ring[0], ring[1], east, west)]
@@ -111,8 +129,9 @@
 
     bi = lax.broadcasted_iota(jnp.int32, (nb, nb), 0)
     bj = lax.broadcasted_iota(jnp.int32, (nb, nb), 1)
-    tcol = own_ref[...]
-    trow = jnp.sum(jnp.where(bi == bj, tcol, 0), axis=0, keepdims=True)
+    trow = own_ref[...]
+    tcol = jnp.sum(jnp.where(bi == bj, trow, 0).astype(F32), axis=1, keepdims=True)
+    tcol = tcol.astype(jnp.int32)
     earlier = jnp.where((tcol == trow) & (bj < bi), 1.0, 0.0)
     place = jnp.sum(earlier, axis=1, keepdims=True).astype(jnp.int32)
     slot = lax.broadcasted_iota(jnp.int32, (nb, 128), 1)
@@ -122,6 +141,25 @@
     to_smem = pltpu.make_async_copy(code_v, code_s, code_sem)
     to_smem.start()
 
+    prod[nb] = jnp.zeros_like(prod[nb])
+    obs = ops.shape[1]
+    observation = lax.broadcasted_iota(jnp.int32, (32, obs), 1)
+
+    def multiply(g, carry):
+        for copy in fetch(g):
+            copy.wait()
+        for i in range(per):
+            b = g * per + i
+            seen = inn_ref[b].astype(F32).reshape(32, obs)
+            seen = jnp.where(observation < count_s[b], seen, 0.0).astype(jnp.bfloat16)
+            p = jnp.dot(seen, ops[b], preferred_element_type=F32)
+            prod[b] = p.astype(jnp.bfloat16).astype(F32)
+        return carry
+
+    lax.fori_loop(0, groups, multiply, 0)
+
+    for copy in state:
+        copy.wait()
     for j in range(4):
         for k in range(4):
             fields[0, j, k] = adj_ref[:, k, j, :]
@@ -155,18 +193,6 @@
     @pl.when(at_high)
     def _():
         lev_hi[...] = jnp.zeros_like(lev_hi)
-
-    prod[nb] = jnp.zeros_like(prod[nb])
-
-    def multiply(g, carry):
-        fetch(g).wait()
-        for i in range(per):
-            b = g * per + i
-            p = jnp.dot(inn_ref[b], ops[b], preferred_element_type=F32)
-            prod[b] = p.astype(jnp.bfloat16).astype(F32)
-        return carry
-
-    lax.fori_loop(0, groups, multiply, 0)
 
     pl.semaphore_wait(barrier, len(greet))
 
@@ -281,14 +307,14 @@
     to_smem.wait()
 
     def tile_sum(tile):
-        total = [jnp.zeros((32, 256), F32) for j in range(4)]
+        rows = [jnp.zeros((32, 256), F32) for j in range(4)]
         for c in range(CAP):
             b = code_s[0, tile * CAP + c]
             row = row_s[jnp.minimum(b, nb - 1)]
             p = prod[b]
             for j in range(4):
-                total[j] = total[j] + p * jnp.where(row == j, 1.0, 0.0)
-        return jnp.concatenate(total, axis=0)
+                rows[j] = rows[j] + p * jnp.where(row == j, 1.0, 0.0)
+        return jnp.concatenate(rows, axis=0)
 
     def ycopy(n):
         return pltpu.make_async_remote_copy(
@@ -404,12 +430,17 @@
     ]
     for copy in finals:
         copy.start()
-    result = fields[STEPS].reshape(128, 256)
-    total = own_part(0, nz - 1) + arrived(0, 0, last) + arrived(0, 1, last)
-    out_ref[:SPLIT] = result[:SPLIT] + total
+    direct = own_part(0, nz - 1) + arrived(0, 0, last) + arrived(0, 1, last)
+    total_lo[:SPLIT], total_hi[:SPLIT] = direct[:, :128], direct[:, 128:]
     for copy in finals:
         copy.wait_recv()
-    out_ref[SPLIT:] = result[SPLIT:] + line[:rest] + decode(frecv[...], fscale_recv[...])
+    crossed = line[:rest] + decode(frecv[...], fscale_recv[...])
+    total_lo[SPLIT:], total_hi[SPLIT:] = crossed[:, :128], crossed[:, 128:]
+    for j in range(4):
+        for k in range(4):
+            pick = pl.ds(j * 32 + k, 8, stride=4)
+            here = jnp.concatenate([total_lo[pick, :], total_hi[pick, :]], axis=1)
+            out_ref[pl.ds((j * 4 + k) * 8, 8)] = fields[STEPS, j, k] + here
 
     for copy in finals:
         copy.wait_send()
@@ -453,27 +484,30 @@
     block_row,
     obs_count,
 ):
-    nb, _, _, obs = innovations.shape
+    nb = innovations.shape[0]
     sizes = tuple(lax.axis_size(name) for name in ("lon", "lat", "lev"))
     nz = sizes[0] // 2
     half = nz // 2
     rest = 128 - SPLIT
-    observed = jnp.arange(obs, dtype=jnp.int32)[None, :] < obs_count[:, None]
-    masked = jnp.where(observed[:, None, None, :], innovations, jnp.zeros((), jnp.bfloat16))
-    masked = masked.transpose(0, 2, 1, 3).reshape(nb, 32, obs)
 
     vmem = pl.BlockSpec(memory_space=pltpu.VMEM)
     smem = pl.BlockSpec(memory_space=pltpu.SMEM)
-    hbm = pl.BlockSpec(memory_space=pl.ANY)
+    hbm = pl.BlockSpec(memory_space=pltpu.HBM)
     dma = pltpu.SemaphoreType.DMA
     i16, bf16, f32 = jnp.int16, jnp.bfloat16, jnp.float32
     out = pl.pallas_call(
         functools.partial(kernel, sizes),
         out_shape=jax.ShapeDtypeStruct((128, 256), f32),
-        in_specs=[smem, smem, smem, vmem, vmem, vmem, vmem, vmem, hbm],
+        in_specs=[smem, smem, smem, smem, vmem, hbm, hbm, hbm, hbm, hbm],
         out_specs=vmem,
         scratch_shapes=[
+            pltpu.VMEM(adjoint_in.shape, f32),
+            pltpu.VMEM(courant_lon.shape, f32),
+            pltpu.VMEM(courant_lat.shape, f32),
+            pltpu.VMEM(innovations.shape, bf16),
             pltpu.VMEM(obs_operator.shape, bf16),
+            dma((3,)),
+            dma((8,)),
             dma((8,)),
             pltpu.VMEM((nb + 1, 32, 256), f32),
             pltpu.VMEM((1, 128), jnp.int32),
@@ -511,20 +545,23 @@
             dma((6, STEPS)),
             dma((6, STEPS)),
             dma((2,)),
+            pltpu.VMEM((128, 128), f32),
+            pltpu.VMEM((128, 128), f32),
         ],
         compiler_params=pltpu.CompilerParams(
-            collective_id=0, has_side_effects=True, vmem_limit_bytes=48 * 2**20
+            collective_id=0, has_side_effects=True, vmem_limit_bytes=60 * 2**20
         ),
         name="adjoint",
     )(
         vert_diff,
         horiz_diff,
         block_row,
+        obs_count,
+        owner_tile.reshape(1, nb),
         adjoint_in,
         courant_lon,
         courant_lat,
-        masked,
-        owner_tile,
+        innovations,
         obs_operator,
     )
     return out.reshape(4, 4, 8, 256).transpose(2, 1, 0, 3)

time: 60.1 us -> 51.7 us (0.86)
  local copies, waits for them, and re-layouts: 8.06 us -> 1.65 us
  other arithmetic: 2.02 us -> 0 us
    unnamed x15 -> x0, local copies, waits for them, and re-layouts: 7.24 us -> none
    transpose x1 -> x0, other arithmetic: 1.29 us -> none  [on_device(): masked = masked.transpose(0, 2, 1, 3).reshape(nb, 32, obs)]
    reshape x1, local copies, waits for them, and re-layouts: 0.74 us -> 1.65 us  [on_device(): return out.reshape(4, 4, 8, 256).transpose(2, 1, 0, 3)]
    lt x1 -> x0, other arithmetic: 0.73 us -> none  [on_device(): observed = jnp.arange(obs, dtype=jnp.int32)[None, :] < obs_count[:, None]]
where the time goes in v2:
time: 51.7 us; the launch traced here: 51.3 us
  Pallas kernels  49.6 us (96%)
  local copies, waits for them, and re-layouts  1.65 us (3%)
    pallas_call x1, Pallas kernels, on_device(): pl.pallas_call(functools.partial(kernel, sizes), out_shape=jax.ShapeDtype...  49.6 us
    reshape x1, local copies, waits for them, and re-layouts, on_device(): return out.reshape(4, 4, 8, 256).transpose(2, 1, 0, 3)  1.65 us

profile of v2, /device:TPU:6, one launch (start us, length us, event | category | flops | bytes accessed | tf_op | source)
XLA Modules:
  0.0 51.3 jit_solution(8233089646703727313)
XLA Ops:
  0.0 49.6 %adjoint.1 = f32[128,256]{1,0:T(8,128)} custom-call(f32[16]{0:T(128)} %vd_s.1, f32[8]{0:T(128)} %hd_s.1, s32[64]{0:T(128)} %row_s.1, s32[64]{0:T(128)} %count_s.1, s32[1,64]{1,0:T(1,128)} %bitcast.6, f32[8,4,4,256]{3,2,1,0:T(4,128)} %adj_hbm.1, f32[4,4,256]{2,1,0:T(4,128)} %cu_hbm.1, f32[4,4,256]{2,1,0:T(4,128)} %cv_hbm.1, bf16[64,8,4,128]{3,2,1,0:T(4,128)(2,1)} %inn_hbm.1, ...), custom_call_target="tpu_custom_call" | custom-call | tf_op jit(solution)/shard_map/adjoint/pallas_call | solution.py:498
  49.6 1.6 %copy.13 = f32[4,4,8,256]{3,0,1,2:T(4,128)} copy(f32[4,4,8,256]{3,2,1,0:T(8,128)} %bitcast.5) | data formatting | bytes 262144 | tf_op jit(solution)/shard_map/reshape | solution.py:567

commit v3 on v2

--- a/solution.py
+++ b/solution.py
@@ -9,10 +9,27 @@
 
 STEPS = 3
 CAP = 4
-SPLIT = 80
 TOP = 32000.0
 MESH = pl.DeviceIdType.MESH
 F32 = jnp.float32
+
+
+def side(reach):
+    parents = {p: p - 1 for p in range(1, min(reach, 3) + 1)}
+    if reach > 3:
+        collector = (reach + 4) // 2
+        parents |= {p: p + 1 for p in range(4, collector)}
+        parents |= {p: p - 1 for p in range(collector + 1, reach + 1)}
+        parents[collector] = 0
+    return parents
+
+
+def tree(nz):
+    parents = side(nz // 2)
+    parents |= {-p: -q for p, q in side(nz // 2 - 1).items()}
+    best = [8, -7, 3, -3, 4, 7, -6, 5, -4, 2, -2, 6, -5, 1, -1, 0]
+    order = [p for p in best if p in parents or p == 0]
+    return parents, order
 
 
 def encode(x):
@@ -56,25 +73,15 @@
     code_s,
     code_sem,
     mine,
-    other,
     ysend,
     yrecv,
     y_sems,
-    asend,
-    arecv,
-    bsend,
-    brecv,
+    zsend,
+    zrecv,
     scale_send,
     scale_recv,
-    ring_send_sem,
-    ring_recv_sem,
-    scale_send_sem,
-    scale_recv_sem,
-    fsend,
-    frecv,
-    fscale_send,
-    fscale_recv,
-    f_sems,
+    z_sems,
+    scale_sems,
     fields,
     lev_lo,
     lev_hi,
@@ -92,12 +99,16 @@
 ):
     n_lon, n_lat, n_lev = sizes
     nz = n_lon // 2
-    half = nz // 2
+    parents, order = tree(nz)
     nb = prod.shape[0] - 1
     lon, lat, lev = (lax.axis_index(name) for name in ("lon", "lat", "lev"))
     z, yl = lon // 2, lon % 2
     partner = z * 2 + (1 - yl)
-    ring = (((z + 1) % nz) * 2 + yl, ((z + nz - 1) % nz) * 2 + yl)
+    sigma = 1 - 2 * (lev % 2)
+
+    def line(offset):
+        return ((z + nz + sigma * offset) % nz) * 2 + yl
+
     east, west = (lon + 1) % n_lon, (lon + n_lon - 1) % n_lon
 
     groups = op_sem.shape[0]
@@ -121,7 +132,10 @@
         copy.start()
 
     barrier = pltpu.get_barrier_semaphore()
-    greet = [{"lon": t} for t in (ring[0], ring[1], east, west)]
+    offsets = {parent - p for p, parent in parents.items()}
+    offsets |= {-offset for offset in offsets}
+    greet = [{"lon": line(offset)} for offset in sorted(offsets)]
+    greet += [{"lon": east}, {"lon": west}]
     greet += [{"lat": (lat + 1) % n_lat}, {"lat": (lat + n_lat - 1) % n_lat}]
     greet += [{"lev": (lev + 1) % n_lev}, {"lev": (lev + n_lev - 1) % n_lev}]
     for target in greet:
@@ -292,17 +306,11 @@
                 fields[r + 1, j, k] = res
 
     def full_step(r):
-        if isinstance(r, int):
-            if r == 0:
-                gated(arrives[1], wind.wait_recv)
-        else:
-            pl.when((r == 0) & ~at_north)(wind.wait_recv)
+        if r == 0:
+            gated(arrives[1], wind.wait_recv)
         sub_step(r)
-        if isinstance(r, int):
-            if r < STEPS - 1:
-                send_halo(r + 1)
-        else:
-            pl.when(r < STEPS - 1)(lambda: send_halo(r + 1))
+        if r < STEPS - 1:
+            send_halo(r + 1)
 
     to_smem.wait()
 
@@ -326,141 +334,70 @@
             device_id_type=MESH,
         )
 
-    def gather(n, carry):
-        away = half - (n + 1) // 2
-        dest = (z + nz + away * (2 * (n % 2) - 1)) % nz
-        theirs = tile_sum(dest * 2 + (1 - yl))
-        ysend[n] = theirs[:SPLIT].astype(jnp.bfloat16)
-        ycopy(n).start()
-        other[n] = theirs[SPLIT:]
-        mine[n] = tile_sum(dest * 2 + yl)
+    def gather(i, carry):
+        place = 0
+        for c, p in enumerate(order):
+            place = jnp.where(i == c, p, place)
+        dest = (z + nz - sigma * place) % nz
+        ysend[i] = tile_sum(dest * 2 + (1 - yl)).astype(jnp.bfloat16)
+        ycopy(i).start()
+        mine[i] = tile_sum(dest * 2 + yl)
         return carry
 
-    def ring_copy(part, way, s):
-        src, dst = ((asend, arecv), (bsend, brecv))[part]
-        q = part * 2 + way
-        data = pltpu.make_async_remote_copy(
-            src_ref=src.at[way, s],
-            dst_ref=dst.at[way, s],
-            send_sem=ring_send_sem.at[q, s],
-            recv_sem=ring_recv_sem.at[q, s],
-            device_id={"lon": ring[way]},
-            device_id_type=MESH,
-        )
-        scale = pltpu.make_async_remote_copy(
-            src_ref=scale_send.at[q, s],
-            dst_ref=scale_recv.at[q, s],
-            send_sem=scale_send_sem.at[q, s],
-            recv_sem=scale_recv_sem.at[q, s],
-            device_id={"lon": ring[way]},
-            device_id_type=MESH,
-        )
-        return data, scale
-
-    def own_part(part, n):
-        if part == 0:
-            ycopy(n).wait_recv()
-            return mine[n, :SPLIT] + yrecv[n].astype(F32)
-        return jnp.concatenate([mine[n, SPLIT:], other[n]], axis=0)
-
-    def arrived(part, way, s):
-        for copy in ring_copy(part, way, s):
-            copy.wait_recv()
-        buf = (arecv, brecv)[part]
-        return decode(buf[way, s], scale_recv[part * 2 + way, s])
-
-    def ring_step(part, way, s, first):
-        n = 2 * s - 1 + way
-        if isinstance(s, int):
-            n = max(n, 0)
-        x = own_part(part, n)
-        if not first:
-            x = x + arrived(part, way, s - 1)
-        ints, scale = encode(x)
-        (asend, bsend)[part][way, s] = ints
-        scale_send[part * 2 + way, s] = scale
-        for copy in ring_copy(part, way, s):
+    lax.fori_loop(0, nz, gather, 0)
+
+    def zcopies(i):
+        p = order[i]
+        target = {"lon": line(parents[p] - p)}
+        return [
+            pltpu.make_async_remote_copy(
+                src_ref=src.at[i],
+                dst_ref=dst.at[i],
+                send_sem=sems.at[0, i],
+                recv_sem=sems.at[1, i],
+                device_id=target,
+                device_id_type=MESH,
+            )
+            for src, dst, sems in (
+                (zsend, zrecv, z_sems),
+                (scale_send, scale_recv, scale_sems),
+            )
+        ]
+
+    def collect(i):
+        ycopy(i).wait_recv()
+        x = mine[i] + yrecv[i].astype(F32)
+        for child, p in enumerate(order):
+            if parents.get(p) == order[i] and p != 0:
+                for copy in zcopies(child):
+                    copy.wait_recv()
+                x = x + decode(zrecv[child], scale_recv[child])
+        return x
+
+    due = {2: 0, 6: 1, 10: 2} if nz == 16 else {0: 0, 1: 1, 2: 2}
+    for i in range(nz - 1):
+        zsend[i], scale_send[i] = encode(collect(i))
+        for copy in zcopies(i):
             copy.start()
-
-    def gather_range(lo, hi):
-        lax.fori_loop(lo, hi, gather, 0)
-
-    gather_range(0, min(5, nz))
-    ring_step(1, 1, 0, True)
-    ring_step(0, 0, 0, True)
-    gather_range(min(5, nz), min(7, nz))
-    ring_step(1, 1, 1, False)
-    ring_step(1, 0, 1, True)
-    ring_step(0, 0, 1, False)
-    ring_step(0, 1, 1, True)
-    gather_range(min(7, nz), min(9, nz))
-
-    def later(s, carry):
-        for part in (1, 0):
-            for way in (0, 1):
-                ring_step(part, way, s, False)
-        lax.fori_loop(jnp.minimum(2 * s + 5, nz), jnp.minimum(2 * s + 7, nz), gather, 0)
-
-        @pl.when((s % 2 == 0) & (s <= 2 * STEPS))
-        def _():
-            full_step(s // 2 - 1)
-
-        return carry
-
-    lax.fori_loop(2, half, later, 0)
-    for r in range(sum(1 for s in range(2, half) if s % 2 == 0 and s <= 2 * STEPS), STEPS):
-        full_step(r)
-
-    last = half - 1
-    line = own_part(1, nz - 1) + arrived(1, 0, last) + arrived(1, 1, last)
-    rest = 128 - SPLIT
-    ints, scale = encode(line[rest:])
-    fsend[...] = ints
-    fscale_send[...] = scale
-    finals = [
-        pltpu.make_async_remote_copy(
-            src_ref=src,
-            dst_ref=dst,
-            send_sem=f_sems.at[q, 0],
-            recv_sem=f_sems.at[q, 1],
-            device_id={"lon": partner},
-            device_id_type=MESH,
-        )
-        for q, (src, dst) in enumerate(((fsend, frecv), (fscale_send, fscale_recv)))
-    ]
-    for copy in finals:
-        copy.start()
-    direct = own_part(0, nz - 1) + arrived(0, 0, last) + arrived(0, 1, last)
-    total_lo[:SPLIT], total_hi[:SPLIT] = direct[:, :128], direct[:, 128:]
-    for copy in finals:
-        copy.wait_recv()
-    crossed = line[:rest] + decode(frecv[...], fscale_recv[...])
-    total_lo[SPLIT:], total_hi[SPLIT:] = crossed[:, :128], crossed[:, 128:]
+        if i in due:
+            full_step(due[i])
+
+    total = collect(nz - 1)
+    total_lo[...], total_hi[...] = total[:, :128], total[:, 128:]
     for j in range(4):
         for k in range(4):
             pick = pl.ds(j * 32 + k, 8, stride=4)
             here = jnp.concatenate([total_lo[pick, :], total_hi[pick, :]], axis=1)
             out_ref[pl.ds((j * 4 + k) * 8, 8)] = fields[STEPS, j, k] + here
 
-    for copy in finals:
-        copy.wait_send()
-
     def y_left(n, carry):
         ycopy(n).wait_send()
         return carry
 
     lax.fori_loop(0, nz, y_left, 0)
 
-    def ring_left(s, carry):
-        for part in range(2):
-            for way in range(2):
-                for copy in ring_copy(part, way, s):
-                    copy.wait_send()
-        return carry
-
-    lax.fori_loop(1, half, ring_left, 0)
-    for part in range(2):
-        for copy in ring_copy(part, part, 0):
+    for i in range(nz - 1):
+        for copy in zcopies(i):
             copy.wait_send()
     gated(sends[1], wind.wait_send)
 
@@ -487,8 +424,6 @@
     nb = innovations.shape[0]
     sizes = tuple(lax.axis_size(name) for name in ("lon", "lat", "lev"))
     nz = sizes[0] // 2
-    half = nz // 2
-    rest = 128 - SPLIT
 
     vmem = pl.BlockSpec(memory_space=pltpu.VMEM)
     smem = pl.BlockSpec(memory_space=pltpu.SMEM)
@@ -514,25 +449,15 @@
             pltpu.SMEM((1, 128), jnp.int32),
             dma,
             pltpu.VMEM((nz, 128, 256), f32),
-            pltpu.VMEM((nz, rest, 256), f32),
-            pltpu.VMEM((nz, SPLIT, 256), bf16),
-            pltpu.VMEM((nz, SPLIT, 256), bf16),
+            pltpu.VMEM((nz, 128, 256), bf16),
+            pltpu.VMEM((nz, 128, 256), bf16),
             dma((2, nz)),
-            pltpu.VMEM((2, half, SPLIT, 256), i16),
-            pltpu.VMEM((2, half, SPLIT, 256), i16),
-            pltpu.VMEM((2, half, 2 * rest, 256), i16),
-            pltpu.VMEM((2, half, 2 * rest, 256), i16),
-            pltpu.VMEM((4, half, 1, 128), f32),
-            pltpu.VMEM((4, half, 1, 128), f32),
-            dma((4, half)),
-            dma((4, half)),
-            dma((4, half)),
-            dma((4, half)),
-            pltpu.VMEM((rest, 256), i16),
-            pltpu.VMEM((rest, 256), i16),
-            pltpu.VMEM((1, 128), f32),
-            pltpu.VMEM((1, 128), f32),
-            dma((2, 2)),
+            pltpu.VMEM((nz - 1, 128, 256), i16),
+            pltpu.VMEM((nz - 1, 128, 256), i16),
+            pltpu.VMEM((nz - 1, 1, 128), f32),
+            pltpu.VMEM((nz - 1, 1, 128), f32),
+            dma((2, nz - 1)),
+            dma((2, nz - 1)),
             pltpu.VMEM((STEPS + 1, 4, 4, 8, 256), f32),
             pltpu.VMEM((STEPS, 4, 8, 256), f32),
             pltpu.VMEM((STEPS, 4, 8, 256), f32),

time: 51.7 us -> 61.5 us (1.19)
  the two profiles are of different devices: /device:TPU:6 before, /device:TPU:1 now
where the time goes in v3:
time: 61.5 us; the launch traced here: 61.4 us
  Pallas kernels  59.7 us (97%)
  local copies, waits for them, and re-layouts  1.65 us (3%)
    pallas_call x1, Pallas kernels, on_device(): pl.pallas_call(functools.partial(kernel, sizes), out_shape=jax.ShapeDtype...  59.7 us
    reshape x1, local copies, waits for them, and re-layouts, on_device(): return out.reshape(4, 4, 8, 256).transpose(2, 1, 0, 3)  1.65 us

profile of v3, /device:TPU:1, one launch (start us, length us, event | category | flops | bytes accessed | tf_op | source)
XLA Modules:
  0.0 61.4 jit_solution(16653843886171960389)
XLA Ops:
  0.0 59.7 %adjoint.1 = f32[128,256]{1,0:T(8,128)} custom-call(f32[16]{0:T(128)} %vd_s.1, f32[8]{0:T(128)} %hd_s.1, s32[64]{0:T(128)} %row_s.1, s32[64]{0:T(128)} %count_s.1, s32[1,64]{1,0:T(1,128)} %bitcast.6, f32[8,4,4,256]{3,2,1,0:T(4,128)} %adj_hbm.1, f32[4,4,256]{2,1,0:T(4,128)} %cu_hbm.1, f32[4,4,256]{2,1,0:T(4,128)} %cv_hbm.1, bf16[64,8,4,128]{3,2,1,0:T(4,128)(2,1)} %inn_hbm.1, ...), custom_call_target="tpu_custom_call" | custom-call | tf_op jit(solution)/shard_map/adjoint/pallas_call | solution.py:433
  59.8 1.6 %copy.13 = f32[4,4,8,256]{3,0,1,2:T(4,128)} copy(f32[4,4,8,256]{3,2,1,0:T(8,128)} %bitcast.5) | data formatting | bytes 262144 | tf_op jit(solution)/shard_map/reshape | solution.py:492

commit v4 on v3

--- a/solution.py
+++ b/solution.py
@@ -27,9 +27,11 @@
 def tree(nz):
     parents = side(nz // 2)
     parents |= {-p: -q for p, q in side(nz // 2 - 1).items()}
-    best = [8, -7, 3, -3, 4, 7, -6, 5, -4, 2, -2, 6, -5, 1, -1, 0]
-    order = [p for p in best if p in parents or p == 0]
-    return parents, order
+    leaves = [p for p, q in parents.items() if p not in parents.values() and abs(p) > abs(q)]
+    leaves.sort(key=abs, reverse=True)
+    best = [4, -4, 5, 7, -6, 6, -5, 2, -2, 1, -1, 0]
+    order = leaves + [p for p in best if p not in leaves and (p in parents or p == 0)]
+    return parents, leaves, order
 
 
 def encode(x):
@@ -73,6 +75,9 @@
     code_s,
     code_sem,
     mine,
+    theirs,
+    lsend,
+    lrecv,
     ysend,
     yrecv,
     y_sems,
@@ -99,7 +104,8 @@
 ):
     n_lon, n_lat, n_lev = sizes
     nz = n_lon // 2
-    parents, order = tree(nz)
+    parents, leaves, order = tree(nz)
+    nl = len(leaves)
     nb = prod.shape[0] - 1
     lon, lat, lev = (lax.axis_index(name) for name in ("lon", "lat", "lev"))
     z, yl = lon // 2, lon % 2
@@ -324,63 +330,94 @@
                 rows[j] = rows[j] + p * jnp.where(row == j, 1.0, 0.0)
         return jnp.concatenate(rows, axis=0)
 
-    def ycopy(n):
-        return pltpu.make_async_remote_copy(
-            src_ref=ysend.at[n],
-            dst_ref=yrecv.at[n],
-            send_sem=y_sems.at[0, n],
-            recv_sem=y_sems.at[1, n],
-            device_id={"lon": partner},
-            device_id_type=MESH,
-        )
-
     def gather(i, carry):
         place = 0
         for c, p in enumerate(order):
             place = jnp.where(i == c, p, place)
         dest = (z + nz - sigma * place) % nz
-        ysend[i] = tile_sum(dest * 2 + (1 - yl)).astype(jnp.bfloat16)
-        ycopy(i).start()
         mine[i] = tile_sum(dest * 2 + yl)
+        theirs[i] = tile_sum(dest * 2 + (1 - yl))
         return carry
 
-    lax.fori_loop(0, nz, gather, 0)
+    def ycopy(i):
+        return pltpu.make_async_remote_copy(
+            src_ref=ysend.at[i - nl],
+            dst_ref=yrecv.at[i - nl],
+            send_sem=y_sems.at[0, i - nl],
+            recv_sem=y_sems.at[1, i - nl],
+            device_id={"lon": partner},
+            device_id_type=MESH,
+        )
 
     def zcopies(i):
         p = order[i]
         target = {"lon": line(parents[p] - p)}
+        if i < nl:
+            data = (lsend.at[i], lrecv.at[i], z_sems)
+        else:
+            data = (zsend.at[i - nl], zrecv.at[i - nl], z_sems)
         return [
             pltpu.make_async_remote_copy(
-                src_ref=src.at[i],
-                dst_ref=dst.at[i],
+                src_ref=src,
+                dst_ref=dst,
                 send_sem=sems.at[0, i],
                 recv_sem=sems.at[1, i],
                 device_id=target,
                 device_id_type=MESH,
             )
-            for src, dst, sems in (
-                (zsend, zrecv, z_sems),
-                (scale_send, scale_recv, scale_sems),
-            )
+            for src, dst, sems in (data, (scale_send.at[i], scale_recv.at[i], scale_sems))
         ]
+
+    def children(i):
+        return [c for c, p in enumerate(order) if p != 0 and parents[p] == order[i]]
+
+    def cross(i):
+        x = theirs[i]
+        for child in children(i):
+            if child < nl:
+                for copy in zcopies(child):
+                    copy.wait_recv()
+                x = x + decode(lrecv[child, 128:], scale_recv[child])
+        ysend[i - nl] = x.astype(jnp.bfloat16)
+        ycopy(i).start()
 
     def collect(i):
         ycopy(i).wait_recv()
-        x = mine[i] + yrecv[i].astype(F32)
-        for child, p in enumerate(order):
-            if parents.get(p) == order[i] and p != 0:
+        x = mine[i] + yrecv[i - nl].astype(F32)
+        for child in children(i):
+            if child < nl:
+                x = x + decode(lrecv[child, :128], scale_recv[child])
+            else:
                 for copy in zcopies(child):
                     copy.wait_recv()
-                x = x + decode(zrecv[child], scale_recv[child])
+                x = x + decode(zrecv[child - nl], scale_recv[child])
         return x
 
-    due = {2: 0, 6: 1, 10: 2} if nz == 16 else {0: 0, 1: 1, 2: 2}
-    for i in range(nz - 1):
-        zsend[i], scale_send[i] = encode(collect(i))
+    lax.fori_loop(0, nl, gather, 0)
+    for i in range(nl):
+        lsend[i], scale_send[i] = encode(jnp.concatenate([mine[i], theirs[i]], axis=0))
         for copy in zcopies(i):
             copy.start()
+    lax.fori_loop(nl, nz, gather, 0)
+
+    crossed = nl
+    due = {nl - 1: 0, nl + 4: 1, nl + 7: 2} if nz == 16 else {nl - 1: 0, nl: 1, nl + 1: 2}
+    for i in range(nl - 1, nz - 1):
+        if i >= nl:
+            zsend[i - nl], scale_send[i] = encode(collect(i))
+            for copy in zcopies(i):
+                copy.start()
+        while crossed < min(nz, i + 4 if i < nl else i + 6):
+            cross(crossed)
+            crossed += 1
         if i in due:
             full_step(due[i])
+    while crossed < nz:
+        cross(crossed)
+        crossed += 1
+    for r in range(STEPS):
+        if r not in [due[i] for i in due if i < nz - 1]:
+            full_step(r)
 
     total = collect(nz - 1)
     total_lo[...], total_hi[...] = total[:, :128], total[:, 128:]
@@ -390,12 +427,8 @@
             here = jnp.concatenate([total_lo[pick, :], total_hi[pick, :]], axis=1)
             out_ref[pl.ds((j * 4 + k) * 8, 8)] = fields[STEPS, j, k] + here
 
-    def y_left(n, carry):
-        ycopy(n).wait_send()
-        return carry
-
-    lax.fori_loop(0, nz, y_left, 0)
-
+    for i in range(nl, nz):
+        ycopy(i).wait_send()
     for i in range(nz - 1):
         for copy in zcopies(i):
             copy.wait_send()
@@ -424,6 +457,7 @@
     nb = innovations.shape[0]
     sizes = tuple(lax.axis_size(name) for name in ("lon", "lat", "lev"))
     nz = sizes[0] // 2
+    nl = len(tree(nz)[1])
 
     vmem = pl.BlockSpec(memory_space=pltpu.VMEM)
     smem = pl.BlockSpec(memory_space=pltpu.SMEM)
@@ -449,11 +483,14 @@
             pltpu.SMEM((1, 128), jnp.int32),
             dma,
             pltpu.VMEM((nz, 128, 256), f32),
-            pltpu.VMEM((nz, 128, 256), bf16),
-            pltpu.VMEM((nz, 128, 256), bf16),
-            dma((2, nz)),
-            pltpu.VMEM((nz - 1, 128, 256), i16),
-            pltpu.VMEM((nz - 1, 128, 256), i16),
+            pltpu.VMEM((nz, 128, 256), f32),
+            pltpu.VMEM((nl, 256, 256), i16),
+            pltpu.VMEM((nl, 256, 256), i16),
+            pltpu.VMEM((nz - nl, 128, 256), bf16),
+            pltpu.VMEM((nz - nl, 128, 256), bf16),
+            dma((2, nz - nl)),
+            pltpu.VMEM((nz - nl, 128, 256), i16),
+            pltpu.VMEM((nz - nl, 128, 256), i16),
             pltpu.VMEM((nz - 1, 1, 128), f32),
             pltpu.VMEM((nz - 1, 1, 128), f32),
             dma((2, nz - 1)),

time: 61.5 us -> 47.9 us (0.78)
  the two profiles are of different devices: /device:TPU:1 before, /device:TPU:6 now
where the time goes in v4:
time: 47.9 us; the launch traced here: 47.7 us
  Pallas kernels  46.1 us (96%)
  local copies, waits for them, and re-layouts  1.65 us (3%)
    pallas_call x1, Pallas kernels, on_device(): pl.pallas_call(functools.partial(kernel, sizes), out_shape=jax.ShapeDtype...  46.1 us
    reshape x1, local copies, waits for them, and re-layouts, on_device(): return out.reshape(4, 4, 8, 256).transpose(2, 1, 0, 3)  1.65 us

profile of v4, /device:TPU:6, one launch (start us, length us, event | category | flops | bytes accessed | tf_op | source)
XLA Modules:
  0.0 47.7 jit_solution(18014913227921412667)
XLA Ops:
  0.0 46.1 %adjoint.1 = f32[128,256]{1,0:T(8,128)} custom-call(f32[16]{0:T(128)} %vd_s.1, f32[8]{0:T(128)} %hd_s.1, s32[64]{0:T(128)} %row_s.1, s32[64]{0:T(128)} %count_s.1, s32[1,64]{1,0:T(1,128)} %bitcast.6, f32[8,4,4,256]{3,2,1,0:T(4,128)} %adj_hbm.1, f32[4,4,256]{2,1,0:T(4,128)} %cu_hbm.1, f32[4,4,256]{2,1,0:T(4,128)} %cv_hbm.1, bf16[64,8,4,128]{3,2,1,0:T(4,128)(2,1)} %inn_hbm.1, ...), custom_call_target="tpu_custom_call" | custom-call | tf_op jit(solution)/shard_map/adjoint/pallas_call | solution.py:467
  46.1 1.6 %copy.13 = f32[4,4,8,256]{3,0,1,2:T(4,128)} copy(f32[4,4,8,256]{3,2,1,0:T(8,128)} %bitcast.5) | data formatting | bytes 262144 | tf_op jit(solution)/shard_map/reshape | solution.py:529

commit v5 on v4

--- a/solution.py
+++ b/solution.py
@@ -29,7 +29,7 @@
     parents |= {-p: -q for p, q in side(nz // 2 - 1).items()}
     leaves = [p for p, q in parents.items() if p not in parents.values() and abs(p) > abs(q)]
     leaves.sort(key=abs, reverse=True)
-    best = [4, -4, 5, 7, -6, 6, -5, 2, -2, 1, -1, 0]
+    best = [8, -7, 4, -4, 3, -3, 5, 7, -6, 6, -5, 2, -2, 1, -1, 0]
     order = leaves + [p for p in best if p not in leaves and (p in parents or p == 0)]
     return parents, leaves, order
 
@@ -51,17 +51,22 @@
 
 def kernel(
     sizes,
-    vd_s,
-    hd_s,
-    row_s,
-    count_s,
-    own_ref,
+    vd_hbm,
+    hd_hbm,
+    row_hbm,
+    count_hbm,
+    own_hbm,
     adj_hbm,
     cu_hbm,
     cv_hbm,
     inn_hbm,
     op_hbm,
     out_ref,
+    vd_s,
+    hd_s,
+    row_s,
+    count_s,
+    own_ref,
     adj_ref,
     cu_ref,
     cv_ref,
@@ -127,10 +132,22 @@
             pltpu.make_async_copy(op_hbm.at[part], ops.at[part], op_sem.at[g]),
         )
 
-    state = [
-        pltpu.make_async_copy(src, dst, in_sems.at[q])
-        for q, (src, dst) in enumerate(((adj_hbm, adj_ref), (cu_hbm, cu_ref), (cv_hbm, cv_ref)))
+    inputs = (
+        (own_hbm, own_ref),
+        (count_hbm, count_s),
+        (row_hbm, row_s),
+        (vd_hbm, vd_s),
+        (hd_hbm, hd_s),
+        (adj_hbm, adj_ref),
+        (cu_hbm, cu_ref),
+        (cv_hbm, cv_ref),
+    )
+    inputs = [
+        pltpu.make_async_copy(src, dst, in_sems.at[q]) for q, (src, dst) in enumerate(inputs)
     ]
+    tables, state = inputs[:5], inputs[5:]
+    for copy in tables:
+        copy.start()
     for g in range(groups):
         for copy in fetch(g):
             copy.start()
@@ -146,6 +163,9 @@
     greet += [{"lev": (lev + 1) % n_lev}, {"lev": (lev + n_lev - 1) % n_lev}]
     for target in greet:
         pl.semaphore_signal(barrier, inc=1, device_id=target, device_id_type=MESH)
+
+    for copy in tables:
+        copy.wait()
 
     bi = lax.broadcasted_iota(jnp.int32, (nb, nb), 0)
     bj = lax.broadcasted_iota(jnp.int32, (nb, nb), 1)
@@ -460,22 +480,39 @@
     nl = len(tree(nz)[1])
 
     vmem = pl.BlockSpec(memory_space=pltpu.VMEM)
-    smem = pl.BlockSpec(memory_space=pltpu.SMEM)
     hbm = pl.BlockSpec(memory_space=pltpu.HBM)
     dma = pltpu.SemaphoreType.DMA
     i16, bf16, f32 = jnp.int16, jnp.bfloat16, jnp.float32
+    operands = (
+        vert_diff,
+        horiz_diff,
+        block_row,
+        obs_count,
+        owner_tile.reshape(1, nb),
+        adjoint_in,
+        courant_lon,
+        courant_lat,
+        innovations,
+        obs_operator,
+    )
+    operands = [pltpu.with_memory_space_constraint(x, pltpu.HBM) for x in operands]
     out = pl.pallas_call(
         functools.partial(kernel, sizes),
         out_shape=jax.ShapeDtypeStruct((128, 256), f32),
-        in_specs=[smem, smem, smem, smem, vmem, hbm, hbm, hbm, hbm, hbm],
+        in_specs=[hbm] * 10,
         out_specs=vmem,
         scratch_shapes=[
+            pltpu.SMEM(vert_diff.shape, f32),
+            pltpu.SMEM(horiz_diff.shape, f32),
+            pltpu.SMEM((nb,), jnp.int32),
+            pltpu.SMEM((nb,), jnp.int32),
+            pltpu.VMEM((1, nb), jnp.int32),
             pltpu.VMEM(adjoint_in.shape, f32),
             pltpu.VMEM(courant_lon.shape, f32),
             pltpu.VMEM(courant_lat.shape, f32),
             pltpu.VMEM(innovations.shape, bf16),
             pltpu.VMEM(obs_operator.shape, bf16),
-            dma((3,)),
+            dma((8,)),
             dma((8,)),
             dma((8,)),
             pltpu.VMEM((nb + 1, 32, 256), f32),
@@ -511,20 +548,11 @@
             pltpu.VMEM((128, 128), f32),
         ],
         compiler_params=pltpu.CompilerParams(
-            collective_id=0, has_side_effects=True, vmem_limit_bytes=60 * 2**20
+            collective_id=0, has_side_effects=True, vmem_limit_bytes=48 * 2**20
         ),
         name="adjoint",
     )(
-        vert_diff,
-        horiz_diff,
-        block_row,
-        obs_count,
-        owner_tile.reshape(1, nb),
-        adjoint_in,
-        courant_lon,
-        courant_lat,
-        innovations,
-        obs_operator,
+        *operands
     )
     return out.reshape(4, 4, 8, 256).transpose(2, 1, 0, 3)
 

time: 47.9 us -> 45.7 us (0.954)
  Pallas kernels: 46.1 us -> 44.8 us
  local copies, waits for them, and re-layouts: 1.65 us -> 0.74 us
    pallas_call x1, Pallas kernels: 46.1 us -> 44.8 us  [on_device(): pl.pallas_call(functools.partial(kernel, sizes), out_shape=jax.ShapeDtype...]
    reshape x1, local copies, waits for them, and re-layouts: 1.65 us -> 0.74 us  [on_device(): return out.reshape(4, 4, 8, 256).transpose(2, 1, 0, 3)]
where the time goes in v5:
time: 45.7 us; the launch traced here: 45.6 us
  Pallas kernels  44.8 us (98%)
  local copies, waits for them, and re-layouts  0.74 us (2%)
    pallas_call x1, Pallas kernels, on_device(): pl.pallas_call(functools.partial(kernel, sizes), out_shape=jax.ShapeDtype...  44.8 us

profile of v5, /device:TPU:6, one launch (start us, length us, event | category | flops | bytes accessed | tf_op | source)
XLA Modules:
  0.0 45.6 jit_solution(15340225200671845995)
XLA Ops:
  0.0 44.8 %adjoint.1 = f32[128,256]{1,0:T(8,128)S(1)} custom-call(f32[16]{0:T(128)} %vd_hbm.1, f32[8]{0:T(128)} %hd_hbm.1, s32[64]{0:T(128)} %row_hbm.1, s32[64]{0:T(128)} %count_hbm.1, s32[1,64]{1,0:T(1,128)} %bitcast.6, f32[8,4,4,256]{3,2,1,0:T(4,128)} %adj_hbm.1, f32[4,4,256]{2,1,0:T(4,128)} %cu_hbm.1, f32[4,4,256]{2,1,0:T(4,128)} %cv_hbm.1, ...), custom_call_target="tpu_custom_call" | custom-call | tf_op jit(solution)/shard_map/adjoint/pallas_call | solution.py:499
  44.8 0.7 %copy.13 = f32[4,4,8,256]{3,0,1,2:T(4,128)} copy(f32[4,4,8,256]{3,2,1,0:T(8,128)S(1)} %bitcast.5) | data formatting | bytes 262144 | tf_op jit(solution)/shard_map/reshape | solution.py:557

commit v6 on v5

--- a/solution.py
+++ b/solution.py
@@ -418,16 +418,18 @@
         lsend[i], scale_send[i] = encode(jnp.concatenate([mine[i], theirs[i]], axis=0))
         for copy in zcopies(i):
             copy.start()
-    lax.fori_loop(nl, nz, gather, 0)
-
-    crossed = nl
+    crossed = min(nl + 3, nz)
+    lax.fori_loop(nl, crossed, gather, 0)
+    for i in range(nl, crossed):
+        cross(i)
+    lax.fori_loop(crossed, nz, gather, 0)
     due = {nl - 1: 0, nl + 4: 1, nl + 7: 2} if nz == 16 else {nl - 1: 0, nl: 1, nl + 1: 2}
     for i in range(nl - 1, nz - 1):
         if i >= nl:
             zsend[i - nl], scale_send[i] = encode(collect(i))
             for copy in zcopies(i):
                 copy.start()
-        while crossed < min(nz, i + 4 if i < nl else i + 6):
+        while crossed < min(nz, i + 4 if i < nl else i + 7):
             cross(crossed)
             crossed += 1
         if i in due:

time: 45.7 us -> 45.1 us (0.987)
  Pallas kernels: 44.8 us -> 44.2 us
    pallas_call x1, Pallas kernels: 44.8 us -> 44.2 us  [on_device(): pl.pallas_call(functools.partial(kernel, sizes), out_shape=jax.ShapeDtype...]
where the time goes in v6:
time: 45.1 us; the launch traced here: 44.9 us
  Pallas kernels  44.2 us (98%)
  local copies, waits for them, and re-layouts  0.74 us (2%)
    pallas_call x1, Pallas kernels, on_device(): pl.pallas_call(functools.partial(kernel, sizes), out_shape=jax.ShapeDtype...  44.2 us

profile of v6, /device:TPU:6, one launch (start us, length us, event | category | flops | bytes accessed | tf_op | source)
XLA Modules:
  0.0 44.9 jit_solution(16385534021070342034)
XLA Ops:
  0.0 44.2 %adjoint.1 = f32[128,256]{1,0:T(8,128)S(1)} custom-call(f32[16]{0:T(128)} %vd_hbm.1, f32[8]{0:T(128)} %hd_hbm.1, s32[64]{0:T(128)} %row_hbm.1, s32[64]{0:T(128)} %count_hbm.1, s32[1,64]{1,0:T(1,128)} %bitcast.6, f32[8,4,4,256]{3,2,1,0:T(4,128)} %adj_hbm.1, f32[4,4,256]{2,1,0:T(4,128)} %cu_hbm.1, f32[4,4,256]{2,1,0:T(4,128)} %cv_hbm.1, ...), custom_call_target="tpu_custom_call" | custom-call | tf_op jit(solution)/shard_map/adjoint/pallas_call | solution.py:501
  44.2 0.7 %copy.13 = f32[4,4,8,256]{3,0,1,2:T(4,128)} copy(f32[4,4,8,256]{3,2,1,0:T(8,128)S(1)} %bitcast.5) | data formatting | bytes 262144 | tf_op jit(solution)/shard_map/reshape | solution.py:559

commit v7 on v6

--- a/solution.py
+++ b/solution.py
@@ -373,9 +373,12 @@
         p = order[i]
         target = {"lon": line(parents[p] - p)}
         if i < nl:
-            data = (lsend.at[i], lrecv.at[i], z_sems)
+            parts = [(lsend.at[i], lrecv.at[i], z_sems)]
         else:
-            data = (zsend.at[i - nl], zrecv.at[i - nl], z_sems)
+            parts = [
+                (zsend.at[i - nl], zrecv.at[i - nl], z_sems),
+                (scale_send.at[i], scale_recv.at[i], scale_sems),
+            ]
         return [
             pltpu.make_async_remote_copy(
                 src_ref=src,
@@ -385,7 +388,7 @@
                 device_id=target,
                 device_id_type=MESH,
             )
-            for src, dst, sems in (data, (scale_send.at[i], scale_recv.at[i], scale_sems))
+            for src, dst, sems in parts
         ]
 
     def children(i):
@@ -397,7 +400,7 @@
             if child < nl:
                 for copy in zcopies(child):
                     copy.wait_recv()
-                x = x + decode(lrecv[child, 128:], scale_recv[child])
+                x = x + lrecv[child, 128:].astype(F32)
         ysend[i - nl] = x.astype(jnp.bfloat16)
         ycopy(i).start()
 
@@ -406,7 +409,7 @@
         x = mine[i] + yrecv[i - nl].astype(F32)
         for child in children(i):
             if child < nl:
-                x = x + decode(lrecv[child, :128], scale_recv[child])
+                x = x + lrecv[child, :128].astype(F32)
             else:
                 for copy in zcopies(child):
                     copy.wait_recv()
@@ -415,7 +418,8 @@
 
     lax.fori_loop(0, nl, gather, 0)
     for i in range(nl):
-        lsend[i], scale_send[i] = encode(jnp.concatenate([mine[i], theirs[i]], axis=0))
+        lsend[i, :128] = mine[i].astype(jnp.bfloat16)
+        lsend[i, 128:] = theirs[i].astype(jnp.bfloat16)
         for copy in zcopies(i):
             copy.start()
     crossed = min(nl + 3, nz)
@@ -523,8 +527,8 @@
             dma,
             pltpu.VMEM((nz, 128, 256), f32),
             pltpu.VMEM((nz, 128, 256), f32),
-            pltpu.VMEM((nl, 256, 256), i16),
-            pltpu.VMEM((nl, 256, 256), i16),
+            pltpu.VMEM((nl, 256, 256), bf16),
+            pltpu.VMEM((nl, 256, 256), bf16),
             pltpu.VMEM((nz - nl, 128, 256), bf16),
             pltpu.VMEM((nz - nl, 128, 256), bf16),
             dma((2, nz - nl)),

time: 45.1 us -> 45.4 us (level); the launches traced: 44.9 us -> 44.7 us
  no operation moved by 1% of the time
where the time goes in v7:
time: 45.4 us; the launch traced here: 44.7 us
  Pallas kernels  44 us (97%)
  local copies, waits for them, and re-layouts  0.74 us (2%)
    pallas_call x1, Pallas kernels, on_device(): pl.pallas_call(functools.partial(kernel, sizes), out_shape=jax.ShapeDtype...  44 us

profile of v7, /device:TPU:6, one launch (start us, length us, event | category | flops | bytes accessed | tf_op | source)
XLA Modules:
  0.0 44.7 jit_solution(10420140858303303162)
XLA Ops:
  0.0 44.0 %adjoint.1 = f32[128,256]{1,0:T(8,128)S(1)} custom-call(f32[16]{0:T(128)} %vd_hbm.1, f32[8]{0:T(128)} %hd_hbm.1, s32[64]{0:T(128)} %row_hbm.1, s32[64]{0:T(128)} %count_hbm.1, s32[1,64]{1,0:T(1,128)} %bitcast.6, f32[8,4,4,256]{3,2,1,0:T(4,128)} %adj_hbm.1, f32[4,4,256]{2,1,0:T(4,128)} %cu_hbm.1, f32[4,4,256]{2,1,0:T(4,128)} %cv_hbm.1, ...), custom_call_target="tpu_custom_call" | custom-call | tf_op jit(solution)/shard_map/adjoint/pallas_call | solution.py:505
  44.0 0.7 %copy.13 = f32[4,4,8,256]{3,0,1,2:T(4,128)} copy(f32[4,4,8,256]{3,2,1,0:T(8,128)S(1)} %bitcast.5) | data formatting | bytes 262144 | tf_op jit(solution)/shard_map/reshape | solution.py:563
